TPU v7x, 32 devices: a whole 2x2x4 slice. The times are simulated.
32 devices in a mesh: grp: 2 (over y), row: 4 (over x, core), col: 4 (over z).
Axes of the slice: x: 2, y: 2, z: 4, core: 2. Of those that a mesh axis runs over, the one named last changes fastest.
Arguments:
- stored: bfloat16 [256, 8192], P(('grp', 'row'), 'col'), parts along dimension 0, may hold values from -6 to 6
- gram_old: float32 [16384, 8192], P(('grp', 'row'), 'col'), parts along dimension 0, may hold values from -4 to 4
- w_enc: bfloat16 [8192, 8192], P('col', 'row'), may hold values from -0.0625 to 0.0625
- b_enc: float32 [8192], P('row'), may hold values from -3 to 3
- b_dec: float32 [8192], P('col'), may hold values from -3 to 3
Outputs:
- gram_new: float32 [16384, 8192], P(('grp', 'row'), 'col'), parts along dimension 0
There are 2 independent parts, one for each index of `grp`. A program takes and returns all parts, laid end to end along the dimension named above; an argument that names none is the same for every part. Nothing has to cross between parts.
All inputs are finite; a program needn't handle non-finite values.
Results may differ from a plain program's by a relative error of at most 0.0012.
Values may be sent and summed in bfloat16 or wider, within the bound.
No kernel may reach another device: no remote copies, remote signals or barrier semaphores. Data moves between devices by JAX's collectives and lax.ppermute only.
A program may use at most 128 MiB of HBM per device.

v0:
```python
import jax
import jax.numpy as jnp
from jax import lax
from jax.sharding import PartitionSpec as P


def spread(value, axis, source):
    kept = jnp.where(lax.axis_index(axis) == source, value, 0).astype(value.dtype)
    return lax.psum(kept, axis)


def shards(stored, gram_old, w_enc, b_enc, b_dec):
    centered = (stored.astype(jnp.float32) - b_dec[None, :]).astype(jnp.bfloat16)
    column = lax.all_gather(centered, "row", axis=0, tiled=True)
    n_col = lax.axis_size("col")
    n_row = lax.axis_size("row")
    partial_sum = jnp.dot(column, w_enc, preferred_element_type=jnp.float32)
    totals = lax.psum(partial_sum, "col")
    panel = jnp.maximum(totals + b_enc[None, :], 0.0).astype(jnp.bfloat16)
    ratio = n_col // n_row
    width_sub = panel.shape[1] // ratio
    col_index = lax.axis_index("col")
    mine = lax.dynamic_slice_in_dim(panel, col_index % ratio * width_sub, width_sub, 1)
    other = spread(mine, "row", col_index // ratio)
    product = lax.dot_general(
        panel, other, (((0,), (0,)), ((), ())), preferred_element_type=jnp.float32
    )
    return gram_old + product / panel.shape[0]


def solution(mesh):
    placed = (
        P(("grp", "row"), "col"),
        P(("grp", "row"), "col"),
        P("col", "row"),
        P("row"),
        P("col"),
    )
    return jax.shard_map(
        shards, mesh=mesh, in_specs=placed, out_specs=P(("grp", "row"), "col"), check_vma=False
    )
```

profile of v0, /device:TPU:0, one launch (start us, length us, event | category | flops | bytes accessed | tf_op | source)
XLA Modules:
  0.0 131.3 jit_solution(12855134411175972922)
XLA Ops:
  6.5 0.0 copy-start
  6.5 0.0 all-reduce.3.cloned.1.call-start
  6.5 0.9 subtract_convert_fusion
  7.5 8.6 %all_gather.3 = bf16[128,2048]{1,0:T(8,128)(2,1)S(1)} all-gather(bf16[32,2048]{1,0:T(8,128)(2,1)S(1)} %subtract_convert_fusion), channel_id=1, replica_groups=mesh['grp'=2,'row'=4,'col'=4] {'row'}, dimensions={0}, use_global_device_ids=true | all-gather | bytes 655360 | tf_op jit(solution)/shard_map/all_gather | solution.py:14
  16.1 5.6 %fusion.1 = f32[128,2048]{1,0:T(8,128)} fusion(bf16[128,2048]{1,0:T(8,128)(2,1)S(1)} %all_gather.3, bf16[2048,2048]{1,0:T(8,128)(2,1)} %param.7), kind=kOutput, calls=%fused_computation.5 | convolution fusion | flops 1073741824 | bytes 9961472 | tf_op jit(solution)/shard_map/dot_general | solution.py:17
  21.7 0.0 all-reduce.3.cloned.1.call-update
  21.8 0.0 all-reduce.5.cloned.1.call-start
  21.8 52.8 %all-reduce.3.cloned.1.call-done = f32[128,2048]{1,0:T(8,128)} async-done(((f32[128,2048]{1,0:T(8,128)}), f32[128,2048]{1,0:T(8,128)}) %all-reduce.3.cloned.1.call-update) | async-done | bytes 1048592 | tf_op jit(solution)/shard_map/psum | solution.py:18
  74.6 0.0 copy-done
  74.6 2.2 %broadcast_select_fusion = bf16[128,2048]{1,0:T(8,128)(2,1)} fusion(pred[]{:T(512)S(6)} %eq.5, f32[128,2048]{1,0:T(8,128)} %all-reduce.3.cloned.1.call-done, f32[2048]{0:T(1024)S(1)} %copy-done), kind=kLoop, calls=%fused_computation.2 | loop fusion | flops 1048576 | bytes 1581057 | tf_op jit(solution)/shard_map/jit(_where)/select_n | solution.py:8
  76.8 0.0 all-reduce.5.cloned.1.call-update
  76.8 32.9 %all-reduce.5.cloned.1.call-done = bf16[128,2048]{1,0:T(8,128)(2,1)} async-done(((bf16[128,2048]{1,0:T(8,128)(2,1)}), bf16[128,2048]{1,0:T(8,128)(2,1)}) %all-reduce.5.cloned.1.call-update) | async-done | bytes 524304 | tf_op jit(solution)/shard_map/psum | solution.py:9
  109.7 14.8 %multiply_add_fusion = f32[2048,2048]{1,0:T(8,128)} fusion(f32[2048,2048]{1,0:T(8,128)} %param.6, bf16[128,2048]{1,0:T(8,128)(2,1)} %all-reduce.5.cloned.1.call-done, f32[128,2048]{1,0:T(8,128)} %all-reduce.3.cloned.1.call-done, f32[2048]{0:T(1024)S(1)} %copy-done), kind=kOutput, calls=%fused_computation | convolution fusion | flops 1082916864 | bytes 35135488 | tf_op jit(solution)/shard_map/dot_general | solution.py:25
Async XLA Ops:
  6.5 68.1 %copy-start = (f32[2048]{0:T(1024)S(1)}, f32[2048]{0:T(1024)}, u32[]{:S(2)}) copy-start(f32[2048]{0:T(1024)} %param.8) | copy-start | bytes 24580
  6.5 68.1 %all-reduce.3.cloned.1.call-start = ((), (), s32[]{:S(2)}) async-start(), calls=%async_computation | async-start | bytes 2097152 | tf_op jit(solution)/shard_map/psum | solution.py:18
  21.8 87.9 %all-reduce.5.cloned.1.call-start = ((), (), s32[]{:S(2)}) async-start(), calls=%async_computation.1 | async-start | bytes 1048576 | tf_op jit(solution)/shard_map/psum | solution.py:9
Sparse Core Ops, SparseCore 0:
  21.9 52.6 all-reduce.2
  77.1 32.5 all-reduce.4
where the time goes:
time: 132 us; the launch traced here: 131 us
  waiting for transfers between devices  85.7 us (65%)
  matrix products  20.4 us (15%)
  between operations  13.4 us (10%)
  blocking collectives  8.62 us (7%)
  other arithmetic  3.09 us (2%)
    psum x1, waiting for transfers between devices, shards(): totals = lax.psum(partial_sum, 'col')  52.8 us
    psum x1, waiting for transfers between devices, spread(): return lax.psum(kept, axis)  32.9 us
    dot_general x1, matrix products, shards(): lax.dot_general(panel, other, (((0,), (0,)), ((), ())), preferred_element...  14.8 us
    all_gather x1, blocking collectives, shards(): column = lax.all_gather(centered, 'row', axis=0, tiled=True)  8.62 us
    dot_general x1, matrix products, shards(): partial_sum = jnp.dot(column, w_enc, preferred_element_type=jnp.float32)  5.64 us
  transfers between devices with their start and end apart: 2, of which 2 were waited for; matrix products, arithmetic and copies ran while one was open for 0% of the time, Pallas kernels for 0%

commit v1 on v0

v1 whole, which is shorter than its diff:
```python
import functools

import jax
import jax.numpy as jnp
from jax import lax
from jax.experimental import pallas as pl
from jax.experimental.pallas import tpu as pltpu
from jax.sharding import PartitionSpec as P

BF16 = jnp.bfloat16
F32 = jnp.float32
CHUNKS = 1
VMEM = pl.BlockSpec(memory_space=pltpu.VMEM)
SMEM = pl.BlockSpec(memory_space=pltpu.SMEM)


def spread(value, axis, source):
    kept = jnp.where(lax.axis_index(axis) == source, value, 0).astype(value.dtype)
    return lax.psum(kept, axis)


def plain(stored, gram_old, w_enc, b_enc, b_dec):
    centered = (stored.astype(F32) - b_dec[None, :]).astype(BF16)
    column = lax.all_gather(centered, "row", axis=0, tiled=True)
    n_col = lax.axis_size("col")
    n_row = lax.axis_size("row")
    partial_sum = jnp.dot(column, w_enc, preferred_element_type=F32)
    totals = lax.psum(partial_sum, "col")
    panel = jnp.maximum(totals + b_enc[None, :], 0.0).astype(BF16)
    ratio = n_col // n_row
    width_sub = panel.shape[1] // ratio
    col_index = lax.axis_index("col")
    mine = lax.dynamic_slice_in_dim(panel, col_index % ratio * width_sub, width_sub, 1)
    other = spread(mine, "row", col_index // ratio)
    product = lax.dot_general(
        panel, other, (((0,), (0,)), ((), ())), preferred_element_type=F32
    )
    return gram_old + product / panel.shape[0]


def flip(value, axis, bit):
    return lax.ppermute(value, axis, [(i, i ^ bit) for i in range(4)])


def center_kernel(at, own, one, two, three, b_dec, out):
    rows = own.shape[0]
    bias = b_dec[...]
    for step, ref in enumerate((own, one, two, three)):
        place = pl.ds(pl.multiple_of((at[0] ^ step) * rows, rows), rows)
        out[place, :] = (ref[...].astype(F32) - bias).astype(BF16)


def center(at, blocks, b_dec):
    rows, depth = blocks[0].shape
    return pl.pallas_call(
        center_kernel,
        out_shape=jax.ShapeDtypeStruct((4 * rows, depth), BF16),
        in_specs=[SMEM] + [VMEM] * 5,
        out_specs=VMEM,
        name="center",
    )(at, *blocks, b_dec[None, :])


def encode_kernel(at, x, w, out):
    out[...] = jnp.dot(x[...], w[...], preferred_element_type=F32).astype(out.dtype)


def encode(piece, x, w, width, dtype):
    rows, depth = x.shape
    tile = min(width, 256)
    per = width // tile
    return pl.pallas_call(
        encode_kernel,
        out_shape=jax.ShapeDtypeStruct((rows, width), dtype),
        grid_spec=pltpu.PrefetchScalarGridSpec(
            num_scalar_prefetch=1,
            grid=(per,),
            in_specs=[
                pl.BlockSpec((rows, depth), lambda j, at: (0, 0)),
                pl.BlockSpec((depth, tile), lambda j, at: (0, at[0] * per + j)),
            ],
            out_specs=pl.BlockSpec((rows, tile), lambda j, at: (0, j)),
        ),
        cost_estimate=pl.CostEstimate(
            flops=2 * rows * depth * width, bytes_accessed=2 * depth * width, transcendentals=0
        ),
        name="encode",
    )(piece, x, w)


def gram_kernel(scale, chunks, at, *refs):
    pieces, (old, out, left, right) = refs[: 4 * chunks], refs[4 * chunks :]
    width = pieces[0].shape[1]
    step = pl.program_id(0)
    tile = out.shape[0]

    @pl.when(step == 0)
    def _():
        for k, ref in enumerate(pieces):
            side, which, chunk = k // (2 * chunks), k // chunks % 2, k % chunks
            index = 2 * chunk + (at[0] ^ which)
            place = pl.ds(pl.multiple_of(index * width, width), width)
            (left, right)[side][:, place] = ref[...]

    rows = left[:, pl.ds(pl.multiple_of(step * tile, tile), tile)]
    product = lax.dot_general(
        rows, right[...], (((0,), (0,)), ((), ())), preferred_element_type=F32
    )
    out[...] = old[...] + product * scale


def gram(half, own, other, own_col, other_col, old):
    chunks = len(own)
    slab, width = own[0].shape
    height, length = old.shape
    tile = 256
    return pl.pallas_call(
        functools.partial(gram_kernel, 1.0 / slab, chunks),
        out_shape=jax.ShapeDtypeStruct(old.shape, F32),
        grid=(height // tile,),
        in_specs=[SMEM] + [VMEM] * (4 * chunks) + [pl.BlockSpec((tile, length), lambda i: (i, 0))],
        out_specs=pl.BlockSpec((tile, length), lambda i: (i, 0)),
        scratch_shapes=[pltpu.VMEM((slab, height), BF16), pltpu.VMEM((slab, length), BF16)],
        compiler_params=pltpu.CompilerParams(vmem_limit_bytes=16 << 20),
        cost_estimate=pl.CostEstimate(
            flops=2 * slab * height * length, bytes_accessed=8 * height * length, transcendentals=0
        ),
        name="gram",
    )(half, *own, *other, *own_col, *other_col, old)


def square(stored, gram_old, w_enc, b_enc, b_dec):
    row, col = lax.axis_index("row"), lax.axis_index("col")
    half = (col & 1).astype(jnp.int32)
    width = w_enc.shape[1] // (2 * CHUNKS)
    one = lambda value: value.astype(jnp.int32)[None]

    across = flip(stored, "row", 2)
    beside = flip(stored, "row", 1)
    slant = flip(across, "row", 1)
    x = center(one(row), (stored, beside, across, slant), b_dec)

    parts = range(CHUNKS)
    mine = [2 * a + half for a in parts]
    theirs = [2 * a + 1 - half for a in parts]
    sent = [flip(encode(one(theirs[a]), x, w_enc, width, BF16), "col", 1) for a in parts]
    kept = [encode(one(mine[a]), x, w_enc, width, F32) for a in parts]
    pair = [kept[a] + sent[a].astype(F32) for a in parts]
    far = [flip(pair[a].astype(BF16), "col", 2) for a in parts]
    bias = [lax.dynamic_slice_in_dim(b_enc, mine[a] * width, width)[None, :] for a in parts]
    own = [
        jnp.maximum(pair[a] + far[a].astype(F32) + bias[a], 0.0).astype(BF16) for a in parts
    ]
    own_x = [flip(own[a], "row", 2) for a in parts]
    other = [flip(own[a], "col", 1) for a in parts]
    other_x = [flip(other[a], "row", 2) for a in parts]

    def column(here, there):
        held = jnp.where(row == col, here, there)
        beside = flip(held, "row", 1)
        return jnp.where((row == col) | ((row ^ 2) == col), held, beside)

    own_col = [column(own[a], own_x[a]) for a in parts]
    other_col = [column(other[a], other_x[a]) for a in parts]
    return gram(one(half), own, other, own_col, other_col, gram_old)


def shards(stored, gram_old, w_enc, b_enc, b_dec):
    if lax.axis_size("row") == 4 and lax.axis_size("col") == 4:
        return square(stored, gram_old, w_enc, b_enc, b_dec)
    return plain(stored, gram_old, w_enc, b_enc, b_dec)


def solution(mesh):
    placed = (
        P(("grp", "row"), "col"),
        P(("grp", "row"), "col"),
        P("col", "row"),
        P("row"),
        P("col"),
    )
    return jax.shard_map(
        shards, mesh=mesh, in_specs=placed, out_specs=P(("grp", "row"), "col"), check_vma=False
    )
```

time: 132 us -> 70.8 us (0.54)
  waiting for transfers between devices: 85.7 us -> 30.5 us
  matrix products: 20.4 us -> 0 us
  Pallas kernels: 0 us -> 19.1 us
  between operations: 13.4 us -> 0.1 us
  starting transfers between devices: 0.04 us -> 11.5 us
  blocking collectives: 8.62 us -> 0 us
  local copies, waits for them, and re-layouts: 0.01 us -> 6.42 us
    psum x2 -> x0, waiting for transfers between devices: 85.7 us -> none  [the longest x1 52.8 us: shards(): totals = lax.psum(partial_sum, 'col')]
    ppermute x0 -> x10, waiting for transfers between devices: none -> 30.5 us  [flip(): return lax.ppermute(value, axis, [(i, i ^ bit) for i in range(4)])]
    dot_general x2 -> x0, matrix products: 20.4 us -> none  [the longest x1 14.8 us: shards(): lax.dot_general(panel, other, (((0,), (0,)), ((), ())), preferred_element...]
    pallas_call x0 -> x4, Pallas kernels: none -> 19.1 us  [the longest x2 9.22 us: encode(): pl.pallas_call(encode_kernel, out_shape=jax.ShapeDtypeStruct((rows, width...]
    ppermute x0 -> x10, starting transfers between devices: none -> 11.5 us  [flip(): return lax.ppermute(value, axis, [(i, i ^ bit) for i in range(4)])]
    all_gather x1 -> x0, blocking collectives: 8.62 us -> none  [shards(): column = lax.all_gather(centered, 'row', axis=0, tiled=True)]
    unnamed x2 -> x10, local copies, waits for them, and re-layouts: 0.01 us -> 6.42 us
    select_n x1 -> x4, other arithmetic: 2.15 us -> 0.12 us  [the longest x2 0.06 us: column(): return jnp.where((row == col) | (row ^ 2 == col), held, beside)]
  transfers between devices with their start and end apart: 2 -> 10, of which waited for: 2 -> 8; matrix products, arithmetic and copies ran while one was open for 0% -> 0% of each run, Pallas kernels for 0% -> 7%
where the time goes in v1:
time: 70.8 us; the launch traced here: 70.1 us
  waiting for transfers between devices  30.5 us (43%)
  Pallas kernels  19.1 us (27%)
  starting transfers between devices  11.5 us (16%)
  local copies, waits for them, and re-layouts  6.42 us (9%)
  other arithmetic  2.38 us (3%)
    ppermute x10, waiting for transfers between devices, flip(): return lax.ppermute(value, axis, [(i, i ^ bit) for i in range(4)])  30.5 us
    ppermute x10, starting transfers between devices, flip(): return lax.ppermute(value, axis, [(i, i ^ bit) for i in range(4)])  11.5 us
    pallas_call x2, Pallas kernels, encode(): pl.pallas_call(encode_kernel, out_shape=jax.ShapeDtypeStruct((rows, width...  9.22 us
    pallas_call x1, Pallas kernels, gram(): pl.pallas_call(functools.partial(gram_kernel, 1.0 / slab, chunks), out_sh...  7.89 us
    unnamed x10, local copies, waits for them, and re-layouts  6.42 us
    pallas_call x1, Pallas kernels, center(): pl.pallas_call(center_kernel, out_shape=jax.ShapeDtypeStruct((4 * rows, d...  1.99 us
  transfers between devices with their start and end apart: 10, of which 8 were waited for; matrix products, arithmetic and copies ran while one was open for 0% of the time, Pallas kernels for 7%

profile of v1, /device:TPU:0, one launch (start us, length us, event | category | flops | bytes accessed | tf_op | source)
XLA Modules:
  0.0 70.1 jit_solution(9741620199504678977)
XLA Ops:
  0.0 2.9 %collective-permute-start.1 = (bf16[32,2048]{1,0:T(8,128)(2,1)}, bf16[32,2048]{1,0:T(8,128)(2,1)S(1)}, u32[]{:S(2)}, u32[]{:S(2)}) collective-permute-start(bf16[32,2048]{1,0:T(8,128)(2,1)} %own.1), channel_id=1, source_target_pairs={{0,8},{4,12},{8,0},{12,4},{1,9},{5,13},{9,1},{13,5},{2,10},{6,14},... | collective-permute-start | bytes 393224 | tf_op jit(solution)/shard_map/ppermute | solution.py:42
  2.9 3.7 %collective-permute-done.1.two = bf16[32,2048]{1,0:T(8,128)(2,1)S(1)} collective-permute-done((bf16[32,2048]{1,0:T(8,128)(2,1)}, bf16[32,2048]{1,0:T(8,128)(2,1)S(1)}, u32[]{:S(2)}, u32[]{:S(2)}) %collective-permute-start.1) | collective-permute-done | bytes 131104 | tf_op jit(solution)/shard_map/ppermute | solution.py:42
  6.7 1.3 %collective-permute-done.2.three = bf16[32,2048]{1,0:T(8,128)(2,1)S(1)} collective-permute-done((bf16[32,2048]{1,0:T(8,128)(2,1)S(1)}, bf16[32,2048]{1,0:T(8,128)(2,1)S(1)}, u32[]{:S(2)}, u32[]{:S(2)}) %collective-permute-start.2) | collective-permute-done | bytes 131104 | tf_op jit(solution)/shard_map/ppermute | solution.py:42
  8.0 0.6 copy-done.3
  8.6 2.0 %center.1.x = bf16[128,2048]{1,0:T(8,128)(2,1)} custom-call(s32[1]{0:T(128)} %bitcast.1.at, bf16[32,2048]{1,0:T(8,128)(2,1)} %own.1, bf16[32,2048]{1,0:T(8,128)(2,1)} %copy-done.2, bf16[32,2048]{1,0:T(8,128)(2,1)} %copy-done.1, bf16[32,2048]{1,0:T(8,128)(2,1)} %copy-done.3, f32[1,2048]{1,0:T(1,128)} %bitcast.4), custom_call_target="tpu_custom_call" | custom-call | tf_op jit(solution)/shard_map/center/pallas_call | solution.py:55
  10.6 4.6 %encode.3 = bf16[128,1024]{1,0:T(8,128)(2,1)} custom-call(s32[1]{0:T(128)} %bitcast.3.at, bf16[128,2048]{1,0:T(8,128)(2,1)} %center.1.x, bf16[2048,2048]{1,0:T(8,128)(2,1)} %w.3), custom_call_target="tpu_custom_call" | custom-call | flops 536870912 | bytes 4194304 | tf_op jit(solution)/shard_map/encode/pallas_call | solution.py:72
  15.2 1.8 %collective-permute-start.3 = (bf16[128,1024]{1,0:T(8,128)(2,1)}, bf16[128,1024]{1,0:T(8,128)(2,1)S(1)}, u32[]{:S(2)}, u32[]{:S(2)}) collective-permute-start(bf16[128,1024]{1,0:T(8,128)(2,1)} %encode.3), channel_id=1, source_target_pairs={{0,1},{1,0},{2,3},{3,2},{4,5},{5,4},{6,7},{7,6},{8,9},{9,8},{10,11... | collective-permute-start | bytes 786440 | tf_op jit(solution)/shard_map/ppermute | solution.py:42
  17.0 4.7 %encode.2 = f32[128,1024]{1,0:T(8,128)} custom-call(s32[1]{0:T(128)} %bitcast.at, bf16[128,2048]{1,0:T(8,128)(2,1)} %center.1.x, bf16[2048,2048]{1,0:T(8,128)(2,1)} %w.3), custom_call_target="tpu_custom_call" | custom-call | flops 536870912 | bytes 4194304 | tf_op jit(solution)/shard_map/encode/pallas_call | solution.py:72
  21.7 2.2 %collective-permute-done.3 = bf16[128,1024]{1,0:T(8,128)(2,1)S(1)} collective-permute-done((bf16[128,1024]{1,0:T(8,128)(2,1)}, bf16[128,1024]{1,0:T(8,128)(2,1)S(1)}, u32[]{:S(2)}, u32[]{:S(2)}) %collective-permute-start.3) | collective-permute-done | bytes 262176 | tf_op jit(solution)/shard_map/ppermute | solution.py:42
  23.9 1.1 %fusion = bf16[128,1024]{1,0:T(8,128)(2,1)S(1)} fusion(f32[128,1024]{1,0:T(8,128)} %encode.2, bf16[128,1024]{1,0:T(8,128)(2,1)S(1)} %collective-permute-done.3), kind=kLoop, calls=%fused_computation.2 | loop fusion | flops 393216 | bytes 1048576 | tf_op jit(solution)/shard_map/convert_element_type | solution.py:149
  25.0 2.8 %collective-permute-start.4 = (bf16[128,1024]{1,0:T(8,128)(2,1)S(1)}, bf16[128,1024]{1,0:T(8,128)(2,1)S(1)}, u32[]{:S(2)}, u32[]{:S(2)}) collective-permute-start(bf16[128,1024]{1,0:T(8,128)(2,1)S(1)} %fusion), channel_id=1, source_target_pairs={{0,2},{1,3},{2,0},{3,1},{4,6},{5,7},{6,4},{7,5},{8,10},{9,11},{10,... | collective-permute-start | bytes 786440 | tf_op jit(solution)/shard_map/ppermute | solution.py:42
  27.8 11.4 %collective-permute-done.4 = bf16[128,1024]{1,0:T(8,128)(2,1)S(1)} collective-permute-done((bf16[128,1024]{1,0:T(8,128)(2,1)S(1)}, bf16[128,1024]{1,0:T(8,128)(2,1)S(1)}, u32[]{:S(2)}, u32[]{:S(2)}) %collective-permute-start.4) | collective-permute-done | bytes 262176 | tf_op jit(solution)/shard_map/ppermute | solution.py:42
  39.2 1.2 %maximum_convert_fusion.refs_0_ = bf16[128,1024]{1,0:T(8,128)(2,1)S(1)} fusion(bf16[128,1024]{1,0:T(8,128)(2,1)S(1)} %collective-permute-done.4, f32[128,1024]{1,0:T(8,128)} %encode.2, bf16[128,1024]{1,0:T(8,128)(2,1)S(1)} %collective-permute-done.3, f32[1024]{0:T(1024)S(1)} %dynamic_slice.3), kind=kLoop, calls=%fused_computation | loop fusion | flops 917504 | bytes 1314816 | tf_op jit(solution)/shard_map/convert_element_type | solution.py:152
  40.4 0.8 %collective-permute-start.5 = (bf16[128,1024]{1,0:T(8,128)(2,1)S(1)}, bf16[128,1024]{1,0:T(8,128)(2,1)S(1)}, u32[]{:S(2)}, u32[]{:S(2)}) collective-permute-start(bf16[128,1024]{1,0:T(8,128)(2,1)S(1)} %maximum_convert_fusion.refs_0_), channel_id=1, source_target_pairs={{0,1},{1,0},{2,3},{3,2},{4,5},{5,4},{6,7},{7,6},{8,9},{9,8},{10,11... | collective-permute-start | bytes 786440 | tf_op jit(solution)/shard_map/ppermute | solution.py:42
  41.1 1.5 %collective-permute-start.6 = (bf16[128,1024]{1,0:T(8,128)(2,1)S(1)}, bf16[128,1024]{1,0:T(8,128)(2,1)S(1)}, u32[]{:S(2)}, u32[]{:S(2)}) collective-permute-start(bf16[128,1024]{1,0:T(8,128)(2,1)S(1)} %maximum_convert_fusion.refs_0_), channel_id=1, source_target_pairs={{0,8},{4,12},{8,0},{12,4},{1,9},{5,13},{9,1},{13,5},{2,10},{6,14},... | collective-permute-start | bytes 786440 | tf_op jit(solution)/shard_map/ppermute | solution.py:42
  42.6 5.0 %collective-permute-done.5.refs_1_ = bf16[128,1024]{1,0:T(8,128)(2,1)S(1)} collective-permute-done((bf16[128,1024]{1,0:T(8,128)(2,1)S(1)}, bf16[128,1024]{1,0:T(8,128)(2,1)S(1)}, u32[]{:S(2)}, u32[]{:S(2)}) %collective-permute-start.5) | collective-permute-done | bytes 262176 | tf_op jit(solution)/shard_map/ppermute | solution.py:42
  47.6 1.5 %collective-permute-start.8 = (bf16[128,1024]{1,0:T(8,128)(2,1)S(1)}, bf16[128,1024]{1,0:T(8,128)(2,1)S(1)}, u32[]{:S(2)}, u32[]{:S(2)}) collective-permute-start(bf16[128,1024]{1,0:T(8,128)(2,1)S(1)} %collective-permute-done.5.refs_1_), channel_id=1, source_target_pairs={{0,8},{4,12},{8,0},{12,4},{1,9},{5,13},{9,1},{13,5},{2,10},{6,14},... | collective-permute-start | bytes 786440 | tf_op jit(solution)/shard_map/ppermute | solution.py:42
  49.1 0.3 collective-permute-done.6
  49.5 0.1 collective-permute-start.7
  49.6 5.1 %collective-permute-done.8 = bf16[128,1024]{1,0:T(8,128)(2,1)S(1)} collective-permute-done((bf16[128,1024]{1,0:T(8,128)(2,1)S(1)}, bf16[128,1024]{1,0:T(8,128)(2,1)S(1)}, u32[]{:S(2)}, u32[]{:S(2)}) %collective-permute-start.8) | collective-permute-done | bytes 262176 | tf_op jit(solution)/shard_map/ppermute | solution.py:42
  54.7 0.1 collective-permute-start.9
  54.9 1.5 %collective-permute-done.9 = bf16[128,1024]{1,0:T(8,128)(2,1)S(1)} collective-permute-done((bf16[128,1024]{1,0:T(8,128)(2,1)S(1)}, bf16[128,1024]{1,0:T(8,128)(2,1)S(1)}, u32[]{:S(2)}, u32[]{:S(2)}) %collective-permute-start.9) | collective-permute-done | bytes 262176 | tf_op jit(solution)/shard_map/ppermute | solution.py:42
  56.4 5.8 %copy-done = f32[2048,2048]{1,0:T(8,128)S(1)} copy-done((f32[2048,2048]{1,0:T(8,128)S(1)}, f32[2048,2048]{1,0:T(8,128)}, u32[]{:S(2)}) %copy-start) | copy-done | bytes 16777240
  62.2 7.9 %gram.1 = f32[2048,2048]{1,0:T(8,128)} custom-call(s32[1]{0:T(128)} %bitcast.at, bf16[128,1024]{1,0:T(8,128)(2,1)S(1)} %maximum_convert_fusion.refs_0_, bf16[128,1024]{1,0:T(8,128)(2,1)S(1)} %collective-permute-done.5.refs_1_, bf16[128,1024]{1,0:T(8,128)(2,1)S(1)} %broadcast_select_fusion.3.refs_2_, bf16[128,1024]{1,0:T(8,128)(2,1)S(1)} %broadcast_select_fusion.2.refs_3_, ...), custom_call_target="tpu_custom_call" | custom-call | flops 1073741824 | bytes 33554432 | tf_op jit(solution)/shard_map/gram/pallas_call | solution.py:117
  (17 shorter events, 0.2 us)
Async XLA Ops:
  0.0 27.8 %copy-start.4 = (f32[2048]{0:T(1024)S(1)}, f32[2048]{0:T(1024)}, u32[]{:S(2)}) copy-start(f32[2048]{0:T(1024)} %param.8) | copy-start | bytes 24580
  0.0 6.6 %collective-permute-start.1 = (bf16[32,2048]{1,0:T(8,128)(2,1)}, bf16[32,2048]{1,0:T(8,128)(2,1)S(1)}, u32[]{:S(2)}, u32[]{:S(2)}) collective-permute-start(bf16[32,2048]{1,0:T(8,128)(2,1)} %own.1), channel_id=1, source_target_pairs={{0,8},{4,12},{8,0},{12,4},{1,9},{5,13},{9,1},{13,5},{2,10},{6,14},... | collective-permute-start | bytes 393224 | tf_op jit(solution)/shard_map/ppermute | solution.py:42
  2.9 3.7 %collective-permute-start = (bf16[32,2048]{1,0:T(8,128)(2,1)}, bf16[32,2048]{1,0:T(8,128)(2,1)S(1)}, u32[]{:S(2)}, u32[]{:S(2)}) collective-permute-start(bf16[32,2048]{1,0:T(8,128)(2,1)} %own.1), channel_id=1, source_target_pairs={{0,4},{4,0},{8,12},{12,8},{1,5},{5,1},{9,13},{13,9},{2,6},{6,2},{1... | collective-permute-start | bytes 393224 | tf_op jit(solution)/shard_map/ppermute | solution.py:42
  6.6 1.4 %copy-start.1 = (bf16[32,2048]{1,0:T(8,128)(2,1)}, bf16[32,2048]{1,0:T(8,128)(2,1)S(1)}, u32[]{:S(2)}) copy-start(bf16[32,2048]{1,0:T(8,128)(2,1)S(1)} %collective-permute-done.1.two) | copy-start | bytes 393220
  6.6 1.3 %collective-permute-start.2 = (bf16[32,2048]{1,0:T(8,128)(2,1)S(1)}, bf16[32,2048]{1,0:T(8,128)(2,1)S(1)}, u32[]{:S(2)}, u32[]{:S(2)}) collective-permute-start(bf16[32,2048]{1,0:T(8,128)(2,1)S(1)} %collective-permute-done.1.two), channel_id=1, source_target_pairs={{0,4},{4,0},{8,12},{12,8},{1,5},{5,1},{9,13},{13,9},{2,6},{6,2},{1... | collective-permute-start | bytes 393224 | tf_op jit(solution)/shard_map/ppermute | solution.py:42
  6.7 1.3 %copy-start.2 = (bf16[32,2048]{1,0:T(8,128)(2,1)}, bf16[32,2048]{1,0:T(8,128)(2,1)S(1)}, u32[]{:S(2)}) copy-start(bf16[32,2048]{1,0:T(8,128)(2,1)S(1)} %collective-permute-done.one) | copy-start | bytes 393220
  8.0 0.7 copy-start.3
  15.2 8.7 %collective-permute-start.3 = (bf16[128,1024]{1,0:T(8,128)(2,1)}, bf16[128,1024]{1,0:T(8,128)(2,1)S(1)}, u32[]{:S(2)}, u32[]{:S(2)}) collective-permute-start(bf16[128,1024]{1,0:T(8,128)(2,1)} %encode.3), channel_id=1, source_target_pairs={{0,1},{1,0},{2,3},{3,2},{4,5},{5,4},{6,7},{7,6},{8,9},{9,8},{10,11... | collective-permute-start | bytes 786440 | tf_op jit(solution)/shard_map/ppermute | solution.py:42
  25.0 14.2 %collective-permute-start.4 = (bf16[128,1024]{1,0:T(8,128)(2,1)S(1)}, bf16[128,1024]{1,0:T(8,128)(2,1)S(1)}, u32[]{:S(2)}, u32[]{:S(2)}) collective-permute-start(bf16[128,1024]{1,0:T(8,128)(2,1)S(1)} %fusion), channel_id=1, source_target_pairs={{0,2},{1,3},{2,0},{3,1},{4,6},{5,7},{6,4},{7,5},{8,10},{9,11},{10,... | collective-permute-start | bytes 786440 | tf_op jit(solution)/shard_map/ppermute | solution.py:42
  40.4 7.3 %collective-permute-start.5 = (bf16[128,1024]{1,0:T(8,128)(2,1)S(1)}, bf16[128,1024]{1,0:T(8,128)(2,1)S(1)}, u32[]{:S(2)}, u32[]{:S(2)}) collective-permute-start(bf16[128,1024]{1,0:T(8,128)(2,1)S(1)} %maximum_convert_fusion.refs_0_), channel_id=1, source_target_pairs={{0,1},{1,0},{2,3},{3,2},{4,5},{5,4},{6,7},{7,6},{8,9},{9,8},{10,11... | collective-permute-start | bytes 786440 | tf_op jit(solution)/shard_map/ppermute | solution.py:42
  41.1 8.3 %collective-permute-start.6 = (bf16[128,1024]{1,0:T(8,128)(2,1)S(1)}, bf16[128,1024]{1,0:T(8,128)(2,1)S(1)}, u32[]{:S(2)}, u32[]{:S(2)}) collective-permute-start(bf16[128,1024]{1,0:T(8,128)(2,1)S(1)} %maximum_convert_fusion.refs_0_), channel_id=1, source_target_pairs={{0,8},{4,12},{8,0},{12,4},{1,9},{5,13},{9,1},{13,5},{2,10},{6,14},... | collective-permute-start | bytes 786440 | tf_op jit(solution)/shard_map/ppermute | solution.py:42
  47.6 7.1 %collective-permute-start.8 = (bf16[128,1024]{1,0:T(8,128)(2,1)S(1)}, bf16[128,1024]{1,0:T(8,128)(2,1)S(1)}, u32[]{:S(2)}, u32[]{:S(2)}) collective-permute-start(bf16[128,1024]{1,0:T(8,128)(2,1)S(1)} %collective-permute-done.5.refs_1_), channel_id=1, source_target_pairs={{0,8},{4,12},{8,0},{12,4},{1,9},{5,13},{9,1},{13,5},{2,10},{6,14},... | collective-permute-start | bytes 786440 | tf_op jit(solution)/shard_map/ppermute | solution.py:42
  49.5 5.3 %collective-permute-start.7 = (bf16[128,1024]{1,0:T(8,128)(2,1)S(1)}, bf16[128,1024]{1,0:T(8,128)(2,1)S(1)}, u32[]{:S(2)}, u32[]{:S(2)}) collective-permute-start(bf16[128,1024]{1,0:T(8,128)(2,1)S(1)} %broadcast_select_fusion.1), channel_id=1, source_target_pairs={{0,4},{4,0},{8,12},{12,8},{1,5},{5,1},{9,13},{13,9},{2,6},{6,2},{1... | collective-permute-start | bytes 786440 | tf_op jit(solution)/shard_map/ppermute | solution.py:42
  54.7 1.6 %collective-permute-start.9 = (bf16[128,1024]{1,0:T(8,128)(2,1)S(1)}, bf16[128,1024]{1,0:T(8,128)(2,1)S(1)}, u32[]{:S(2)}, u32[]{:S(2)}) collective-permute-start(bf16[128,1024]{1,0:T(8,128)(2,1)S(1)} %broadcast_select_fusion), channel_id=1, source_target_pairs={{0,4},{4,0},{8,12},{12,8},{1,5},{5,1},{9,13},{13,9},{2,6},{6,2},{1... | collective-permute-start | bytes 786440 | tf_op jit(solution)/shard_map/ppermute | solution.py:42
  56.4 5.8 %copy-start = (f32[2048,2048]{1,0:T(8,128)S(1)}, f32[2048,2048]{1,0:T(8,128)}, u32[]{:S(2)}) copy-start(f32[2048,2048]{1,0:T(8,128)} %refs_4_.1) | copy-start | bytes 50331652

commit v2 on v0

v2 whole, which is shorter than its diff:
```python
import jax
import jax.numpy as jnp
from jax import lax
from jax.experimental import pallas as pl
from jax.experimental.pallas import tpu as pltpu
from jax.sharding import PartitionSpec as P

BF16 = jnp.bfloat16
F32 = jnp.float32
MIB = 1 << 20
VMEM = pl.BlockSpec(memory_space=pltpu.VMEM)
SMEM = pl.BlockSpec(memory_space=pltpu.SMEM)
ANY = pl.BlockSpec(memory_space=pl.ANY)


def spread(value, axis, source):
    kept = jnp.where(lax.axis_index(axis) == source, value, 0).astype(value.dtype)
    return lax.psum(kept, axis)


def plain(stored, gram_old, w_enc, b_enc, b_dec):
    centered = (stored.astype(F32) - b_dec[None, :]).astype(BF16)
    column = lax.all_gather(centered, "row", axis=0, tiled=True)
    n_col = lax.axis_size("col")
    n_row = lax.axis_size("row")
    partial_sum = jnp.dot(column, w_enc, preferred_element_type=F32)
    totals = lax.psum(partial_sum, "col")
    panel = jnp.maximum(totals + b_enc[None, :], 0.0).astype(BF16)
    ratio = n_col // n_row
    width_sub = panel.shape[1] // ratio
    col_index = lax.axis_index("col")
    mine = lax.dynamic_slice_in_dim(panel, col_index % ratio * width_sub, width_sub, 1)
    other = spread(mine, "row", col_index // ratio)
    product = lax.dot_general(
        panel, other, (((0,), (0,)), ((), ())), preferred_element_type=F32
    )
    return gram_old + product / panel.shape[0]


def flip(value, axis, bit):
    return lax.ppermute(value, axis, [(i, i ^ bit) for i in range(4)])


def in_hbm(value):
    return pltpu.with_memory_space_constraint(value, pltpu.HBM)


def in_vmem(value):
    return pltpu.with_memory_space_constraint(value, pltpu.VMEM)


def params(mib):
    return pltpu.CompilerParams(vmem_limit_bytes=mib * MIB)


def cost(flops, moved):
    return pl.CostEstimate(flops=flops, bytes_accessed=moved, transcendentals=0)


def struct(shape, dtype):
    return jax.ShapeDtypeStruct(shape, dtype)


TILE = 256
DEPTH_TILE = 512


def row_and_col():
    return lax.axis_index("row"), lax.axis_index("col")


def window(start, size):
    return pl.ds(pl.multiple_of(start, size), size)


def center_into(x, core, here, beside, b_dec):
    rows = here.shape[0]
    for bit, ref in ((0, here), (1, beside)):
        place = window((core ^ bit) * rows, rows)
        x[place, :] = (ref[...].astype(F32) - b_dec[...]).astype(BF16)


def start_loads(half, w, held, sems):
    width = held.shape[1]
    copies = []
    for j in range(held.shape[0] // DEPTH_TILE):
        place = pl.ds(j * DEPTH_TILE, DEPTH_TILE)
        source = w.at[place, window(half * width, width)]
        copies.append(pltpu.make_async_copy(source, held.at[place, :], sems.at[j]))
        copies[-1].start()
    return copies


def dot_as_loaded(copies, x, held):
    total = None
    for j, copy in enumerate(copies):
        copy.wait()
        place = pl.ds(j * DEPTH_TILE, DEPTH_TILE)
        product = jnp.dot(x[:, place], held[place, :], preferred_element_type=F32)
        total = product if total is None else total + product
    return total


def first_send_kernel(here, beside, b_dec, w, out, x, held, sems):
    row, col = row_and_col()
    copies = start_loads(1 - (col & 1), w, held, sems)
    center_into(x, row & 1, here, beside, b_dec)
    out[...] = dot_as_loaded(copies, x, held).astype(BF16)


def first_keep_kernel(x, w, out, held, sems):
    _, col = row_and_col()
    out[...] = dot_as_loaded(start_loads(col & 1, w, held, sems), x, held)


def first_send(here, beside, b_dec, w):
    rows, depth, width = 2 * here.shape[0], here.shape[1], w.shape[1] // 2
    return pl.pallas_call(
        first_send_kernel,
        out_shape=(
            struct((rows, width), BF16),
            struct((rows, depth), BF16),
            struct((depth, width), BF16),
        ),
        in_specs=[VMEM, VMEM, VMEM, ANY],
        out_specs=(VMEM, VMEM, VMEM),
        scratch_shapes=[pltpu.SemaphoreType.DMA((depth // DEPTH_TILE,))],
        compiler_params=params(4),
        cost_estimate=cost(2 * rows * depth * width, 2 * depth * width),
        name="first_send",
    )(here, beside, b_dec, in_hbm(w))


def first_keep(x, w):
    rows, depth, width = x.shape[0], x.shape[1], w.shape[1] // 2
    return pl.pallas_call(
        first_keep_kernel,
        out_shape=(struct((rows, width), F32), struct((depth, width), BF16)),
        in_specs=[VMEM, ANY],
        out_specs=(VMEM, VMEM),
        scratch_shapes=[pltpu.SemaphoreType.DMA((depth // DEPTH_TILE,))],
        compiler_params=params(4),
        cost_estimate=cost(2 * rows * depth * width, 2 * depth * width),
        name="first_keep",
    )(x, in_hbm(w))


def dot_tiles(x, held, out):
    for j in range(out.shape[1] // TILE):
        place = pl.ds(j * TILE, TILE)
        product = jnp.dot(x[...], held[:, place], preferred_element_type=F32)
        out[:, place] = product.astype(out.dtype)


def next_send_kernel(here, beside, b_dec, held, out, x):
    center_into(x, row_and_col()[0] & 1, here, beside, b_dec)
    dot_tiles(x, held, out)


def next_send(here, beside, b_dec, held):
    rows, (depth, width) = 2 * here.shape[0], held.shape
    return pl.pallas_call(
        next_send_kernel,
        out_shape=(struct((rows, width), BF16), struct((rows, depth), BF16)),
        in_specs=[VMEM] * 4,
        out_specs=(VMEM, VMEM),
        compiler_params=params(4),
        cost_estimate=cost(2 * rows * depth * width, 2 * rows * depth),
        name="next_send",
    )(here, beside, b_dec, in_vmem(held))


def next_keep(x, held):
    rows, (depth, width) = x.shape[0], held.shape
    return pl.pallas_call(
        dot_tiles,
        out_shape=struct((rows, width), F32),
        in_specs=[VMEM, VMEM],
        out_specs=VMEM,
        compiler_params=params(4),
        cost_estimate=cost(2 * rows * depth * width, 2 * rows * depth),
        name="next_keep",
    )(x, in_vmem(held))


def small(kernel, name, shape, *operands):
    return pl.pallas_call(
        kernel,
        out_shape=struct(shape, BF16),
        in_specs=[VMEM] * len(operands),
        out_specs=VMEM,
        compiler_params=params(2),
        name=name,
    )(*operands)


def pair_kernel(kept, sent, out):
    out[...] = (kept[...] + sent[...].astype(F32)).astype(BF16)


def codes_kernel(kept, sent, far, b_enc, out):
    width = out.shape[1]
    bias = b_enc[:, window((row_and_col()[1] & 1) * width, width)]
    total = kept[...] + sent[...].astype(F32) + far[...].astype(F32) + bias
    out[...] = jnp.maximum(total, 0.0).astype(BF16)


def choose_kernel(here, there, out):
    row, col = row_and_col()

    @pl.when(row == col)
    def _():
        out[...] = here[...]

    @pl.when(row != col)
    def _():
        out[...] = there[...]


def load_kernel(_, source, out, sem):
    copy = pltpu.make_async_copy(source, out, sem)
    copy.start()
    copy.wait()


def load(after, source):
    return pl.pallas_call(
        load_kernel,
        out_shape=struct(source.shape, source.dtype),
        in_specs=[ANY, ANY],
        out_specs=VMEM,
        scratch_shapes=[pltpu.SemaphoreType.DMA(())],
        compiler_params=params(1),
        cost_estimate=cost(0, 4 * source.size),
        name="load",
    )(after, in_hbm(source))


def gram_kernel(*refs):
    pieces, (old, out, left, right, new, sems) = refs[:12], refs[12:]
    rows, width = pieces[0].shape
    row, col = row_and_col()
    held = (row == col) | ((row ^ 2) == col)
    for k in range(4):
        chunk, other = k // 2, k % 2
        half = window(((col & 1) ^ other) * width, width)
        left[window(((row >> 1) ^ chunk) * rows, rows), half] = pieces[k][...]
        place = window(((col >> 1) ^ chunk) * rows, rows)

        @pl.when(held)
        def _():
            right[place, half] = pieces[4 + k][...]

        @pl.when(jnp.logical_not(held))
        def _():
            right[place, half] = pieces[8 + k][...]

    scale = 1.0 / left.shape[0]
    copies = []
    for i in range(out.shape[0] // TILE):
        tile = pl.ds(i * TILE, TILE)
        product = lax.dot_general(
            left[:, tile], right[...], (((0,), (0,)), ((), ())), preferred_element_type=F32
        )
        new[tile, :] = old[tile, :] + product * scale
        copies.append(pltpu.make_async_copy(new.at[tile, :], out.at[tile, :], sems.at[i]))
        copies[-1].start()
    for copy in copies:
        copy.wait()


def gram(own, held, passed, old):
    height, length = old.shape
    slab = 2 * own[0].shape[0]
    return pl.pallas_call(
        gram_kernel,
        out_shape=struct(old.shape, F32),
        in_specs=[VMEM] * 13,
        out_specs=ANY,
        scratch_shapes=[
            pltpu.VMEM((slab, height), BF16),
            pltpu.VMEM((slab, length), BF16),
            pltpu.VMEM(old.shape, F32),
            pltpu.SemaphoreType.DMA((height // TILE,)),
        ],
        compiler_params=params(24),
        cost_estimate=cost(2 * slab * height * length, 8 * height * length),
        name="gram",
    )(*own, *held, *passed, in_vmem(old))


def after(value, other):
    return lax.optimization_barrier((value, other))[0]


def square(stored, gram_old, w_enc, b_enc, b_dec):
    b_dec, b_enc = b_dec[None, :], b_enc[None, :]

    beside = flip(stored, "row", 1)
    across = flip(stored, "row", 2)
    out_a, x_a, w_out = first_send(stored, beside, b_dec, w_enc)
    sent_a = flip(out_a, "col", 1)
    kept_a, w_keep = first_keep(x_a, w_enc)
    across = after(across, kept_a)
    slant = flip(across, "row", 1)
    out_b, x_b = next_send(across, slant, b_dec, w_out)
    shape = out_a.shape

    def pair_sum(kept, sent):
        return small(pair_kernel, "pair_sum", shape, kept, sent)

    pair_a = pair_sum(kept_a, sent_a)
    sent_b = flip(after(out_b, pair_a), "col", 1)
    far_a = flip(pair_a, "col", 2)
    kept_b = next_keep(x_b, w_keep)
    old = load(pair_a, gram_old)
    pair_b = pair_sum(kept_b, sent_b)
    far_b = flip(after(pair_b, old), "col", 2)

    def finish(kept, sent, far):
        own = small(codes_kernel, "codes", shape, kept, sent, far, b_enc)
        other = flip(own, "col", 1)
        own_x = flip(own, "row", 2)
        other_x = flip(other, "row", 2)
        held_own = small(choose_kernel, "choose", shape, own, own_x)
        held_other = small(choose_kernel, "choose", shape, other, other_x)
        return [own, other], [held_own, held_other]

    far_a = after(far_a, old)
    own_a, held_a = finish(kept_a, sent_a, far_a)
    own_b, held_b = finish(kept_b, sent_b, far_b)
    held = held_a + held_b
    passed = [flip(piece, "row", 1) for piece in held]
    return gram(own_a + own_b, held, passed, old)


def shards(stored, gram_old, w_enc, b_enc, b_dec):
    if lax.axis_size("row") == 4 and lax.axis_size("col") == 4:
        return square(stored, gram_old, w_enc, b_enc, b_dec)
    return plain(stored, gram_old, w_enc, b_enc, b_dec)


def solution(mesh):
    placed = (
        P(("grp", "row"), "col"),
        P(("grp", "row"), "col"),
        P("col", "row"),
        P("row"),
        P("col"),
    )
    return jax.shard_map(
        shards, mesh=mesh, in_specs=placed, out_specs=P(("grp", "row"), "col"), check_vma=False
    )
```

time: 132 us -> 54.1 us (0.41)
  waiting for transfers between devices: 85.7 us -> 17.7 us
  matrix products: 20.4 us -> 0 us
  Pallas kernels: 0 us -> 19.2 us
  starting transfers between devices: 0.04 us -> 15.1 us
  between operations: 13.4 us -> 0.22 us
  blocking collectives: 8.62 us -> 0 us
  other arithmetic: 3.09 us -> 0 us
  local copies, waits for them, and re-layouts: 0.01 us -> 1.64 us
    psum x2 -> x0, waiting for transfers between devices: 85.7 us -> none  [the longest x1 52.8 us: shards(): totals = lax.psum(partial_sum, 'col')]
    dot_general x2 -> x0, matrix products: 20.4 us -> none  [the longest x1 14.8 us: shards(): lax.dot_general(panel, other, (((0,), (0,)), ((), ())), preferred_element...]
    pallas_call x0 -> x14, Pallas kernels: none -> 19.2 us  [the longest x1 6.48 us: gram(): pl.pallas_call(gram_kernel, out_shape=struct(old.shape, F32), in_specs=[V...]
    ppermute x0 -> x17, waiting for transfers between devices: none -> 17.7 us  [flip(): return lax.ppermute(value, axis, [(i, i ^ bit) for i in range(4)])]
    ppermute x0 -> x17, starting transfers between devices: none -> 15.1 us  [flip(): return lax.ppermute(value, axis, [(i, i ^ bit) for i in range(4)])]
    all_gather x1 -> x0, blocking collectives: 8.62 us -> none  [shards(): column = lax.all_gather(centered, 'row', axis=0, tiled=True)]
    select_n x1 -> x0, other arithmetic: 2.15 us -> none  [spread(): jnp.where(lax.axis_index(axis) == source, value, 0).astype(value.dtype)]
    unnamed x2 -> x8, local copies, waits for them, and re-layouts: 0.01 us -> 1.64 us
  transfers between devices with their start and end apart: 2 -> 17, of which waited for: 2 -> 8; matrix products, arithmetic and copies ran while one was open for 0% -> 0% of each run, Pallas kernels for 0% -> 22%
where the time goes in v2:
time: 54.1 us; the launch traced here: 53.9 us
  Pallas kernels  19.2 us (35%)
  waiting for transfers between devices  17.7 us (33%)
  starting transfers between devices  15.1 us (28%)
  local copies, waits for them, and re-layouts  1.64 us (3%)
    ppermute x17, waiting for transfers between devices, flip(): return lax.ppermute(value, axis, [(i, i ^ bit) for i in range(4)])  17.7 us
    ppermute x17, starting transfers between devices, flip(): return lax.ppermute(value, axis, [(i, i ^ bit) for i in range(4)])  15.1 us
    pallas_call x1, Pallas kernels, gram(): pl.pallas_call(gram_kernel, out_shape=struct(old.shape, F32), in_specs=[V...  6.48 us
    pallas_call x1, Pallas kernels, load(): pl.pallas_call(load_kernel, out_shape=struct(source.shape, source.dtype),...  5.78 us
    pallas_call x1, Pallas kernels, first_send(): pl.pallas_call(first_send_kernel, out_shape=(struct((rows, width), BF16),...  2.52 us
    pallas_call x1, Pallas kernels, first_keep(): pl.pallas_call(first_keep_kernel, out_shape=(struct((rows, width), F32),...  2.5 us
    unnamed x8, local copies, waits for them, and re-layouts  1.64 us
  transfers between devices with their start and end apart: 17, of which 8 were waited for; matrix products, arithmetic and copies ran while one was open for 0% of the time, Pallas kernels for 22%

profile of v2, /device:TPU:0, one launch (start us, length us, event | category | flops | bytes accessed | tf_op | source)
XLA Modules:
  0.0 53.9 jit_solution(6286982559106479275)
XLA Ops:
  0.5 2.5 %collective-permute-start.4 = (bf16[32,2048]{1,0:T(8,128)(2,1)}, bf16[32,2048]{1,0:T(8,128)(2,1)S(1)}, u32[]{:S(2)}, u32[]{:S(2)}) collective-permute-start(bf16[32,2048]{1,0:T(8,128)(2,1)} %here.1), channel_id=1, source_target_pairs={{0,8},{4,12},{8,0},{12,4},{1,9},{5,13},{9,1},{13,5},{2,10},{6,14},... | collective-permute-start | bytes 393224 | tf_op jit(solution)/shard_map/ppermute | solution.py:41
  2.9 0.9 %copy-done = bf16[32,2048]{1,0:T(8,128)(2,1)S(1)} copy-done((bf16[32,2048]{1,0:T(8,128)(2,1)S(1)}, bf16[32,2048]{1,0:T(8,128)(2,1)}, u32[]{:S(2)}) %copy-start) | copy-done | bytes 131096
  3.9 0.7 %copy-done.1 = f32[2048]{0:T(1024)S(1)} copy-done((f32[2048]{0:T(1024)S(1)}, f32[2048]{0:T(1024)}, u32[]{:S(2)}) %copy-start.1) | copy-done | bytes 8216
  4.6 2.5 %first_send.1 = (bf16[64,1024]{1,0:T(8,128)(2,1)S(1)}, bf16[64,2048]{1,0:T(8,128)(2,1)S(1)}, bf16[2048,1024]{1,0:T(8,128)(2,1)S(1)}) custom-call(bf16[32,2048]{1,0:T(8,128)(2,1)S(1)} %copy-done, bf16[32,2048]{1,0:T(8,128)(2,1)S(1)} %collective-permute-done.beside, f32[1,2048]{1,0:T(1,128)S(1)} %bitcast.2, bf16[2048,2048]{1,0:T(8,128)(2,1)} %w.3), custom_call_target="tpu_custom_call" | custom-call | flops 268435456 | bytes 4194304 | tf_op jit(solution)/shard_map/first_send/pallas_call | solution.py:118
  7.1 1.7 %collective-permute-start.1 = (bf16[64,1024]{1,0:T(8,128)(2,1)S(1)}, bf16[64,1024]{1,0:T(8,128)(2,1)S(1)}, u32[]{:S(2)}, u32[]{:S(2)}) collective-permute-start(bf16[64,1024]{1,0:T(8,128)(2,1)S(1)} %get-tuple-element.18), channel_id=1, source_target_pairs={{0,1},{1,0},{2,3},{3,2},{4,5},{5,4},{6,7},{7,6},{8,9},{9,8},{10,11... | collective-permute-start | bytes 393224 | tf_op jit(solution)/shard_map/ppermute | solution.py:41
  8.8 2.5 %first_keep.1 = (f32[64,1024]{1,0:T(8,128)S(1)}, bf16[2048,1024]{1,0:T(8,128)(2,1)S(1)}) custom-call(bf16[64,2048]{1,0:T(8,128)(2,1)S(1)} %get-tuple-element.16.x, bf16[2048,2048]{1,0:T(8,128)(2,1)} %w.3), custom_call_target="tpu_custom_call" | custom-call | flops 268435456 | bytes 4194304 | tf_op jit(solution)/shard_map/first_keep/pallas_call | solution.py:136
  11.4 1.4 %collective-permute-done.1.sent = bf16[64,1024]{1,0:T(8,128)(2,1)S(1)} collective-permute-done((bf16[64,1024]{1,0:T(8,128)(2,1)S(1)}, bf16[64,1024]{1,0:T(8,128)(2,1)S(1)}, u32[]{:S(2)}, u32[]{:S(2)}) %collective-permute-start.1) | collective-permute-done | bytes 131104 | tf_op jit(solution)/shard_map/ppermute | solution.py:41
  12.9 0.9 %next_send.1 = (bf16[64,1024]{1,0:T(8,128)(2,1)S(1)}, bf16[64,2048]{1,0:T(8,128)(2,1)S(1)}) custom-call(bf16[32,2048]{1,0:T(8,128)(2,1)S(1)} %collective-permute-done.4.here, bf16[32,2048]{1,0:T(8,128)(2,1)S(1)} %collective-permute-done.5.beside, f32[1,2048]{1,0:T(1,128)S(1)} %bitcast.3, bf16[2048,1024]{1,0:T(8,128)(2,1)S(1)} %get-tuple-element.21.held), custom_call_target="tpu_custom_call" | custom-call | flops 268435456 | bytes 262144 | tf_op jit(solution)/shard_map/next_send/pallas_call | solution.py:162
  13.8 1.6 %collective-permute-start.6 = (bf16[64,1024]{1,0:T(8,128)(2,1)S(1)}, bf16[64,1024]{1,0:T(8,128)(2,1)S(1)}, u32[]{:S(2)}, u32[]{:S(2)}) collective-permute-start(bf16[64,1024]{1,0:T(8,128)(2,1)S(1)} %get-tuple-element.25), channel_id=1, source_target_pairs={{0,1},{1,0},{2,3},{3,2},{4,5},{5,4},{6,7},{7,6},{8,9},{9,8},{10,11... | collective-permute-start | bytes 393224 | tf_op jit(solution)/shard_map/ppermute | solution.py:41
  15.4 2.6 %collective-permute-start.2 = (bf16[64,1024]{1,0:T(8,128)(2,1)S(1)}, bf16[64,1024]{1,0:T(8,128)(2,1)S(1)}, u32[]{:S(2)}, u32[]{:S(2)}) collective-permute-start(bf16[64,1024]{1,0:T(8,128)(2,1)S(1)} %pair_sum.2._), channel_id=1, source_target_pairs={{0,2},{1,3},{2,0},{3,1},{4,6},{5,7},{6,4},{7,5},{8,10},{9,11},{10,... | collective-permute-start | bytes 393224 | tf_op jit(solution)/shard_map/ppermute | solution.py:41
  18.0 0.8 %next_keep.1.kept = f32[64,1024]{1,0:T(8,128)S(1)} custom-call(bf16[64,2048]{1,0:T(8,128)(2,1)S(1)} %get-tuple-element.22.x, bf16[2048,1024]{1,0:T(8,128)(2,1)S(1)} %get-tuple-element.23.held), custom_call_target="tpu_custom_call" | custom-call | flops 268435456 | bytes 262144 | tf_op jit(solution)/shard_map/next_keep/pallas_call | solution.py:175
  18.8 5.8 %load.1.refs_12_ = f32[2048,2048]{1,0:T(8,128)S(1)} custom-call(bf16[64,1024]{1,0:T(8,128)(2,1)S(1)} %pair_sum.2._, f32[2048,2048]{1,0:T(8,128)} %source.1), custom_call_target="tpu_custom_call" | custom-call | bytes 16777216 | tf_op jit(solution)/shard_map/load/pallas_call | solution.py:227
  25.2 0.5 collective-permute-start.3
  25.7 7.0 %collective-permute-done.7.far = bf16[64,1024]{1,0:T(8,128)(2,1)S(1)} collective-permute-done((bf16[64,1024]{1,0:T(8,128)(2,1)S(1)}, bf16[64,1024]{1,0:T(8,128)(2,1)S(1)}, u32[]{:S(2)}, u32[]{:S(2)}) %collective-permute-start.7) | collective-permute-done | bytes 131104 | tf_op jit(solution)/shard_map/ppermute | solution.py:41
  32.8 1.5 %collective-permute-start.9 = (bf16[64,1024]{1,0:T(8,128)(2,1)S(1)}, bf16[64,1024]{1,0:T(8,128)(2,1)S(1)}, u32[]{:S(2)}, u32[]{:S(2)}) collective-permute-start(bf16[64,1024]{1,0:T(8,128)(2,1)S(1)} %codes.2.here.refs_0_), channel_id=1, source_target_pairs={{0,8},{4,12},{8,0},{12,4},{1,9},{5,13},{9,1},{13,5},{2,10},{6,14},... | collective-permute-start | bytes 393224 | tf_op jit(solution)/shard_map/ppermute | solution.py:41
  34.3 0.6 %collective-permute-start.10 = (bf16[64,1024]{1,0:T(8,128)(2,1)S(1)}, bf16[64,1024]{1,0:T(8,128)(2,1)S(1)}, u32[]{:S(2)}, u32[]{:S(2)}) collective-permute-start(bf16[64,1024]{1,0:T(8,128)(2,1)S(1)} %collective-permute-done.3.here.refs_1_), channel_id=1, source_target_pairs={{0,8},{4,12},{8,0},{12,4},{1,9},{5,13},{9,1},{13,5},{2,10},{6,14},... | collective-permute-start | bytes 393224 | tf_op jit(solution)/shard_map/ppermute | solution.py:41
  34.9 1.4 %collective-permute-start.11 = (bf16[64,1024]{1,0:T(8,128)(2,1)S(1)}, bf16[64,1024]{1,0:T(8,128)(2,1)S(1)}, u32[]{:S(2)}, u32[]{:S(2)}) collective-permute-start(bf16[64,1024]{1,0:T(8,128)(2,1)S(1)} %codes.3.here.refs_2_), channel_id=1, source_target_pairs={{0,8},{4,12},{8,0},{12,4},{1,9},{5,13},{9,1},{13,5},{2,10},{6,14},... | collective-permute-start | bytes 393224 | tf_op jit(solution)/shard_map/ppermute | solution.py:41
  36.3 1.5 %collective-permute-done.8.here.refs_3_ = bf16[64,1024]{1,0:T(8,128)(2,1)S(1)} collective-permute-done((bf16[64,1024]{1,0:T(8,128)(2,1)S(1)}, bf16[64,1024]{1,0:T(8,128)(2,1)S(1)}, u32[]{:S(2)}, u32[]{:S(2)}) %collective-permute-start.8) | collective-permute-done | bytes 131104 | tf_op jit(solution)/shard_map/ppermute | solution.py:41
  37.8 1.4 %collective-permute-start.12 = (bf16[64,1024]{1,0:T(8,128)(2,1)S(1)}, bf16[64,1024]{1,0:T(8,128)(2,1)S(1)}, u32[]{:S(2)}, u32[]{:S(2)}) collective-permute-start(bf16[64,1024]{1,0:T(8,128)(2,1)S(1)} %collective-permute-done.8.here.refs_3_), channel_id=1, source_target_pairs={{0,8},{4,12},{8,0},{12,4},{1,9},{5,13},{9,1},{13,5},{2,10},{6,14},... | collective-permute-start | bytes 393224 | tf_op jit(solution)/shard_map/ppermute | solution.py:41
  39.4 2.7 %collective-permute-done.10.there = bf16[64,1024]{1,0:T(8,128)(2,1)S(1)} collective-permute-done((bf16[64,1024]{1,0:T(8,128)(2,1)S(1)}, bf16[64,1024]{1,0:T(8,128)(2,1)S(1)}, u32[]{:S(2)}, u32[]{:S(2)}) %collective-permute-start.10) | collective-permute-done | bytes 131104 | tf_op jit(solution)/shard_map/ppermute | solution.py:41
  42.2 2.4 %collective-permute-done.11.there = bf16[64,1024]{1,0:T(8,128)(2,1)S(1)} collective-permute-done((bf16[64,1024]{1,0:T(8,128)(2,1)S(1)}, bf16[64,1024]{1,0:T(8,128)(2,1)S(1)}, u32[]{:S(2)}, u32[]{:S(2)}) %collective-permute-start.11) | collective-permute-done | bytes 131104 | tf_op jit(solution)/shard_map/ppermute | solution.py:41
  44.7 1.3 %collective-permute-done.12.there = bf16[64,1024]{1,0:T(8,128)(2,1)S(1)} collective-permute-done((bf16[64,1024]{1,0:T(8,128)(2,1)S(1)}, bf16[64,1024]{1,0:T(8,128)(2,1)S(1)}, u32[]{:S(2)}, u32[]{:S(2)}) %collective-permute-start.12) | collective-permute-done | bytes 131104 | tf_op jit(solution)/shard_map/ppermute | solution.py:41
  46.1 1.3 %collective-permute-done.16.refs_11_ = bf16[64,1024]{1,0:T(8,128)(2,1)S(1)} collective-permute-done((bf16[64,1024]{1,0:T(8,128)(2,1)S(1)}, bf16[64,1024]{1,0:T(8,128)(2,1)S(1)}, u32[]{:S(2)}, u32[]{:S(2)}) %collective-permute-start.16) | collective-permute-done | bytes 131104 | tf_op jit(solution)/shard_map/ppermute | solution.py:41
  47.4 6.5 %gram.1 = f32[2048,2048]{1,0:T(8,128)} custom-call(bf16[64,1024]{1,0:T(8,128)(2,1)S(1)} %codes.2.here.refs_0_, bf16[64,1024]{1,0:T(8,128)(2,1)S(1)} %collective-permute-done.3.here.refs_1_, bf16[64,1024]{1,0:T(8,128)(2,1)S(1)} %codes.3.here.refs_2_, bf16[64,1024]{1,0:T(8,128)(2,1)S(1)} %collective-permute-done.8.here.refs_3_, ...), custom_call_target="tpu_custom_call" | custom-call | flops 1073741824 | bytes 33554432 | tf_op jit(solution)/shard_map/gram/pallas_call | solution.py:275
  (32 shorter events, 1.7 us)
Async XLA Ops:
  0.0 2.9 %collective-permute-start = (bf16[32,2048]{1,0:T(8,128)(2,1)}, bf16[32,2048]{1,0:T(8,128)(2,1)S(1)}, u32[]{:S(2)}, u32[]{:S(2)}) collective-permute-start(bf16[32,2048]{1,0:T(8,128)(2,1)} %here.1), channel_id=1, source_target_pairs={{0,4},{4,0},{8,12},{12,8},{1,5},{5,1},{9,13},{13,9},{2,6},{6,2},{1... | collective-permute-start | bytes 393224 | tf_op jit(solution)/shard_map/ppermute | solution.py:41
  0.5 10.8 %collective-permute-start.4 = (bf16[32,2048]{1,0:T(8,128)(2,1)}, bf16[32,2048]{1,0:T(8,128)(2,1)S(1)}, u32[]{:S(2)}, u32[]{:S(2)}) collective-permute-start(bf16[32,2048]{1,0:T(8,128)(2,1)} %here.1), channel_id=1, source_target_pairs={{0,8},{4,12},{8,0},{12,4},{1,9},{5,13},{9,1},{13,5},{2,10},{6,14},... | collective-permute-start | bytes 393224 | tf_op jit(solution)/shard_map/ppermute | solution.py:41
  2.9 0.9 %copy-start = (bf16[32,2048]{1,0:T(8,128)(2,1)S(1)}, bf16[32,2048]{1,0:T(8,128)(2,1)}, u32[]{:S(2)}) copy-start(bf16[32,2048]{1,0:T(8,128)(2,1)} %here.1) | copy-start | bytes 393220
  3.9 0.7 %copy-start.1 = (f32[2048]{0:T(1024)S(1)}, f32[2048]{0:T(1024)}, u32[]{:S(2)}) copy-start(f32[2048]{0:T(1024)} %param.9) | copy-start | bytes 24580
  4.6 8.3 %copy-start.2 = (f32[2048]{0:T(1024)S(1)}, f32[2048]{0:T(1024)}, u32[]{:S(2)}) copy-start(f32[2048]{0:T(1024)} %param.9) | copy-start | bytes 24580
  7.1 5.7 %collective-permute-start.1 = (bf16[64,1024]{1,0:T(8,128)(2,1)S(1)}, bf16[64,1024]{1,0:T(8,128)(2,1)S(1)}, u32[]{:S(2)}, u32[]{:S(2)}) collective-permute-start(bf16[64,1024]{1,0:T(8,128)(2,1)S(1)} %get-tuple-element.18), channel_id=1, source_target_pairs={{0,1},{1,0},{2,3},{3,2},{4,5},{5,4},{6,7},{7,6},{8,9},{9,8},{10,11... | collective-permute-start | bytes 393224 | tf_op jit(solution)/shard_map/ppermute | solution.py:41
  11.3 1.5 %collective-permute-start.5 = (bf16[32,2048]{1,0:T(8,128)(2,1)S(1)}, bf16[32,2048]{1,0:T(8,128)(2,1)S(1)}, u32[]{:S(2)}, u32[]{:S(2)}) collective-permute-start(bf16[32,2048]{1,0:T(8,128)(2,1)S(1)} %collective-permute-done.4.here), channel_id=1, source_target_pairs={{0,4},{4,0},{8,12},{12,8},{1,5},{5,1},{9,13},{13,9},{2,6},{6,2},{1... | collective-permute-start | bytes 393224 | tf_op jit(solution)/shard_map/ppermute | solution.py:41
  13.8 10.9 %collective-permute-start.6 = (bf16[64,1024]{1,0:T(8,128)(2,1)S(1)}, bf16[64,1024]{1,0:T(8,128)(2,1)S(1)}, u32[]{:S(2)}, u32[]{:S(2)}) collective-permute-start(bf16[64,1024]{1,0:T(8,128)(2,1)S(1)} %get-tuple-element.25), channel_id=1, source_target_pairs={{0,1},{1,0},{2,3},{3,2},{4,5},{5,4},{6,7},{7,6},{8,9},{9,8},{10,11... | collective-permute-start | bytes 393224 | tf_op jit(solution)/shard_map/ppermute | solution.py:41
  15.4 9.7 %collective-permute-start.2 = (bf16[64,1024]{1,0:T(8,128)(2,1)S(1)}, bf16[64,1024]{1,0:T(8,128)(2,1)S(1)}, u32[]{:S(2)}, u32[]{:S(2)}) collective-permute-start(bf16[64,1024]{1,0:T(8,128)(2,1)S(1)} %pair_sum.2._), channel_id=1, source_target_pairs={{0,2},{1,3},{2,0},{3,1},{4,6},{5,7},{6,4},{7,5},{8,10},{9,11},{10,... | collective-permute-start | bytes 393224 | tf_op jit(solution)/shard_map/ppermute | solution.py:41
  18.8 6.3 %copy-start.3 = (f32[2048]{0:T(1024)S(1)}, f32[2048]{0:T(1024)}, u32[]{:S(2)}) copy-start(f32[2048]{0:T(1024)} %param.8) | copy-start | bytes 24580
  24.7 8.0 %collective-permute-start.7 = (bf16[64,1024]{1,0:T(8,128)(2,1)S(1)}, bf16[64,1024]{1,0:T(8,128)(2,1)S(1)}, u32[]{:S(2)}, u32[]{:S(2)}) collective-permute-start(bf16[64,1024]{1,0:T(8,128)(2,1)S(1)} %pair_sum.3), channel_id=1, source_target_pairs={{0,2},{1,3},{2,0},{3,1},{4,6},{5,7},{6,4},{7,5},{8,10},{9,11},{10,... | collective-permute-start | bytes 393224 | tf_op jit(solution)/shard_map/ppermute | solution.py:41
  25.2 9.1 %collective-permute-start.3 = (bf16[64,1024]{1,0:T(8,128)(2,1)S(1)}, bf16[64,1024]{1,0:T(8,128)(2,1)S(1)}, u32[]{:S(2)}, u32[]{:S(2)}) collective-permute-start(bf16[64,1024]{1,0:T(8,128)(2,1)S(1)} %codes.2.here.refs_0_), channel_id=1, source_target_pairs={{0,1},{1,0},{2,3},{3,2},{4,5},{5,4},{6,7},{7,6},{8,9},{9,8},{10,11... | collective-permute-start | bytes 393224 | tf_op jit(solution)/shard_map/ppermute | solution.py:41
  32.7 5.0 %collective-permute-start.8 = (bf16[64,1024]{1,0:T(8,128)(2,1)S(1)}, bf16[64,1024]{1,0:T(8,128)(2,1)S(1)}, u32[]{:S(2)}, u32[]{:S(2)}) collective-permute-start(bf16[64,1024]{1,0:T(8,128)(2,1)S(1)} %codes.3.here.refs_2_), channel_id=1, source_target_pairs={{0,1},{1,0},{2,3},{3,2},{4,5},{5,4},{6,7},{7,6},{8,9},{9,8},{10,11... | collective-permute-start | bytes 393224 | tf_op jit(solution)/shard_map/ppermute | solution.py:41
  32.8 6.5 %collective-permute-start.9 = (bf16[64,1024]{1,0:T(8,128)(2,1)S(1)}, bf16[64,1024]{1,0:T(8,128)(2,1)S(1)}, u32[]{:S(2)}, u32[]{:S(2)}) collective-permute-start(bf16[64,1024]{1,0:T(8,128)(2,1)S(1)} %codes.2.here.refs_0_), channel_id=1, source_target_pairs={{0,8},{4,12},{8,0},{12,4},{1,9},{5,13},{9,1},{13,5},{2,10},{6,14},... | collective-permute-start | bytes 393224 | tf_op jit(solution)/shard_map/ppermute | solution.py:41
  34.3 7.8 %collective-permute-start.10 = (bf16[64,1024]{1,0:T(8,128)(2,1)S(1)}, bf16[64,1024]{1,0:T(8,128)(2,1)S(1)}, u32[]{:S(2)}, u32[]{:S(2)}) collective-permute-start(bf16[64,1024]{1,0:T(8,128)(2,1)S(1)} %collective-permute-done.3.here.refs_1_), channel_id=1, source_target_pairs={{0,8},{4,12},{8,0},{12,4},{1,9},{5,13},{9,1},{13,5},{2,10},{6,14},... | collective-permute-start | bytes 393224 | tf_op jit(solution)/shard_map/ppermute | solution.py:41
  34.9 9.7 %collective-permute-start.11 = (bf16[64,1024]{1,0:T(8,128)(2,1)S(1)}, bf16[64,1024]{1,0:T(8,128)(2,1)S(1)}, u32[]{:S(2)}, u32[]{:S(2)}) collective-permute-start(bf16[64,1024]{1,0:T(8,128)(2,1)S(1)} %codes.3.here.refs_2_), channel_id=1, source_target_pairs={{0,8},{4,12},{8,0},{12,4},{1,9},{5,13},{9,1},{13,5},{2,10},{6,14},... | collective-permute-start | bytes 393224 | tf_op jit(solution)/shard_map/ppermute | solution.py:41
  37.8 8.2 %collective-permute-start.12 = (bf16[64,1024]{1,0:T(8,128)(2,1)S(1)}, bf16[64,1024]{1,0:T(8,128)(2,1)S(1)}, u32[]{:S(2)}, u32[]{:S(2)}) collective-permute-start(bf16[64,1024]{1,0:T(8,128)(2,1)S(1)} %collective-permute-done.8.here.refs_3_), channel_id=1, source_target_pairs={{0,8},{4,12},{8,0},{12,4},{1,9},{5,13},{9,1},{13,5},{2,10},{6,14},... | collective-permute-start | bytes 393224 | tf_op jit(solution)/shard_map/ppermute | solution.py:41
  39.3 6.8 %collective-permute-start.13 = (bf16[64,1024]{1,0:T(8,128)(2,1)S(1)}, bf16[64,1024]{1,0:T(8,128)(2,1)S(1)}, u32[]{:S(2)}, u32[]{:S(2)}) collective-permute-start(bf16[64,1024]{1,0:T(8,128)(2,1)S(1)} %choose.4.refs_4_), channel_id=1, source_target_pairs={{0,4},{4,0},{8,12},{12,8},{1,5},{5,1},{9,13},{13,9},{2,6},{6,2},{1... | collective-permute-start | bytes 393224 | tf_op jit(solution)/shard_map/ppermute | solution.py:41
  42.1 4.0 %collective-permute-start.14 = (bf16[64,1024]{1,0:T(8,128)(2,1)S(1)}, bf16[64,1024]{1,0:T(8,128)(2,1)S(1)}, u32[]{:S(2)}, u32[]{:S(2)}) collective-permute-start(bf16[64,1024]{1,0:T(8,128)(2,1)S(1)} %choose.5.refs_5_), channel_id=1, source_target_pairs={{0,4},{4,0},{8,12},{12,8},{1,5},{5,1},{9,13},{13,9},{2,6},{6,2},{1... | collective-permute-start | bytes 393224 | tf_op jit(solution)/shard_map/ppermute | solution.py:41
  44.6 1.5 %collective-permute-start.15 = (bf16[64,1024]{1,0:T(8,128)(2,1)S(1)}, bf16[64,1024]{1,0:T(8,128)(2,1)S(1)}, u32[]{:S(2)}, u32[]{:S(2)}) collective-permute-start(bf16[64,1024]{1,0:T(8,128)(2,1)S(1)} %choose.6.refs_6_), channel_id=1, source_target_pairs={{0,4},{4,0},{8,12},{12,8},{1,5},{5,1},{9,13},{13,9},{2,6},{6,2},{1... | collective-permute-start | bytes 393224 | tf_op jit(solution)/shard_map/ppermute | solution.py:41
  46.0 1.4 %collective-permute-start.16 = (bf16[64,1024]{1,0:T(8,128)(2,1)S(1)}, bf16[64,1024]{1,0:T(8,128)(2,1)S(1)}, u32[]{:S(2)}, u32[]{:S(2)}) collective-permute-start(bf16[64,1024]{1,0:T(8,128)(2,1)S(1)} %choose.7.refs_7_), channel_id=1, source_target_pairs={{0,4},{4,0},{8,12},{12,8},{1,5},{5,1},{9,13},{13,9},{2,6},{6,2},{1... | collective-permute-start | bytes 393224 | tf_op jit(solution)/shard_map/ppermute | solution.py:41

commit v3 on v2

--- a/solution.py
+++ b/solution.py
@@ -1,3 +1,5 @@
+import functools
+
 import jax
 import jax.numpy as jnp
 from jax import lax
@@ -63,6 +65,7 @@
 
 TILE = 256
 DEPTH_TILE = 512
+GRAM_TILE = 128
 
 
 def row_and_col():
@@ -101,34 +104,41 @@
     return total
 
 
-def first_send_kernel(here, beside, b_dec, w, out, x, held, sems):
-    row, col = row_and_col()
-    copies = start_loads(1 - (col & 1), w, held, sems)
-    center_into(x, row & 1, here, beside, b_dec)
-    out[...] = dot_as_loaded(copies, x, held).astype(BF16)
-
-
 def first_keep_kernel(x, w, out, held, sems):
     _, col = row_and_col()
     out[...] = dot_as_loaded(start_loads(col & 1, w, held, sems), x, held)
 
 
-def first_send(here, beside, b_dec, w):
-    rows, depth, width = 2 * here.shape[0], here.shape[1], w.shape[1] // 2
-    return pl.pallas_call(
-        first_send_kernel,
+def load_first_kernel(stored, b_dec, w, stored_out, b_dec_out, held, sems, own_sems):
+    own = [
+        pltpu.make_async_copy(stored, stored_out, own_sems.at[0]),
+        pltpu.make_async_copy(b_dec, b_dec_out, own_sems.at[1]),
+    ]
+    for copy in own:
+        copy.start()
+    for copy in start_loads(1 - (row_and_col()[1] & 1), w, held, sems) + own:
+        copy.wait()
+
+
+def load_first(stored, b_dec, w):
+    depth, width = w.shape[0], w.shape[1] // 2
+    return pl.pallas_call(
+        load_first_kernel,
         out_shape=(
-            struct((rows, width), BF16),
-            struct((rows, depth), BF16),
+            struct(stored.shape, BF16),
+            struct(b_dec.shape, F32),
             struct((depth, width), BF16),
         ),
-        in_specs=[VMEM, VMEM, VMEM, ANY],
-        out_specs=(VMEM, VMEM, VMEM),
-        scratch_shapes=[pltpu.SemaphoreType.DMA((depth // DEPTH_TILE,))],
-        compiler_params=params(4),
-        cost_estimate=cost(2 * rows * depth * width, 2 * depth * width),
-        name="first_send",
-    )(here, beside, b_dec, in_hbm(w))
+        in_specs=[ANY] * 3,
+        out_specs=(VMEM,) * 3,
+        scratch_shapes=[
+            pltpu.SemaphoreType.DMA((depth // DEPTH_TILE,)),
+            pltpu.SemaphoreType.DMA((2,)),
+        ],
+        compiler_params=params(1),
+        cost_estimate=cost(0, 2 * depth * width),
+        name="load_first",
+    )(in_hbm(stored), in_hbm(b_dec), in_hbm(w))
 
 
 def first_keep(x, w):
@@ -152,25 +162,25 @@
         out[:, place] = product.astype(out.dtype)
 
 
-def next_send_kernel(here, beside, b_dec, held, out, x):
+def send_kernel(here, beside, b_dec, held, out, x):
     center_into(x, row_and_col()[0] & 1, here, beside, b_dec)
     dot_tiles(x, held, out)
 
 
-def next_send(here, beside, b_dec, held):
+def send(here, beside, b_dec, held):
     rows, (depth, width) = 2 * here.shape[0], held.shape
     return pl.pallas_call(
-        next_send_kernel,
+        send_kernel,
         out_shape=(struct((rows, width), BF16), struct((rows, depth), BF16)),
         in_specs=[VMEM] * 4,
         out_specs=(VMEM, VMEM),
         compiler_params=params(4),
         cost_estimate=cost(2 * rows * depth * width, 2 * rows * depth),
-        name="next_send",
+        name="send",
     )(here, beside, b_dec, in_vmem(held))
 
 
-def next_keep(x, held):
+def keep(x, held):
     rows, (depth, width) = x.shape[0], held.shape
     return pl.pallas_call(
         dot_tiles,
@@ -179,7 +189,7 @@
         out_specs=VMEM,
         compiler_params=params(4),
         cost_estimate=cost(2 * rows * depth * width, 2 * rows * depth),
-        name="next_keep",
+        name="keep",
     )(x, in_vmem(held))
 
 
@@ -217,121 +227,138 @@
         out[...] = there[...]
 
 
-def load_kernel(_, source, out, sem):
-    copy = pltpu.make_async_copy(source, out, sem)
+def load_kernel(part, _, source, out, sem):
+    rows = out.shape[0]
+    copy = pltpu.make_async_copy(source.at[pl.ds(part * rows, rows), :], out, sem)
     copy.start()
     copy.wait()
 
 
-def load(after, source):
-    return pl.pallas_call(
-        load_kernel,
-        out_shape=struct(source.shape, source.dtype),
+def load_half(part, ready, source):
+    rows, columns = source.shape[0] // 2, source.shape[1]
+    return pl.pallas_call(
+        functools.partial(load_kernel, part),
+        out_shape=struct((rows, columns), source.dtype),
         in_specs=[ANY, ANY],
         out_specs=VMEM,
         scratch_shapes=[pltpu.SemaphoreType.DMA(())],
         compiler_params=params(1),
-        cost_estimate=cost(0, 4 * source.size),
-        name="load",
-    )(after, in_hbm(source))
-
-
-def gram_kernel(*refs):
-    pieces, (old, out, left, right, new, sems) = refs[:12], refs[12:]
+        cost_estimate=cost(0, 16 * rows * columns),
+        name="load_half",
+    )(ready, in_hbm(source))
+
+
+def gram_kernel(other, *refs):
+    pieces, olds, (out, left, right, new, sems) = refs[:8], refs[8:10], refs[-5:]
     rows, width = pieces[0].shape
     row, col = row_and_col()
     held = (row == col) | ((row ^ 2) == col)
     for k in range(4):
-        chunk, other = k // 2, k % 2
-        half = window(((col & 1) ^ other) * width, width)
+        chunk = k // 2
+        half = window(((col & 1) ^ (k % 2)) * width, width)
         left[window(((row >> 1) ^ chunk) * rows, rows), half] = pieces[k][...]
+    for chunk in range(2):
         place = window(((col >> 1) ^ chunk) * rows, rows)
 
         @pl.when(held)
         def _():
-            right[place, half] = pieces[4 + k][...]
+            right[place, :] = pieces[4 + chunk][...]
 
         @pl.when(jnp.logical_not(held))
         def _():
-            right[place, half] = pieces[8 + k][...]
+            right[place, :] = pieces[6 + chunk][...]
 
     scale = 1.0 / left.shape[0]
+    columns = window(((col & 1) ^ other) * width, width)
     copies = []
-    for i in range(out.shape[0] // TILE):
-        tile = pl.ds(i * TILE, TILE)
+    tiles = out.shape[0] // GRAM_TILE
+    for i in range(tiles):
+        tile = pl.ds(i * GRAM_TILE, GRAM_TILE)
+        old, place = olds[i * 2 // tiles], pl.ds(i % (tiles // 2) * GRAM_TILE, GRAM_TILE)
         product = lax.dot_general(
             left[:, tile], right[...], (((0,), (0,)), ((), ())), preferred_element_type=F32
         )
-        new[tile, :] = old[tile, :] + product * scale
-        copies.append(pltpu.make_async_copy(new.at[tile, :], out.at[tile, :], sems.at[i]))
+        new[tile, :] = old[place, columns] + product * scale
+        copies.append(
+            pltpu.make_async_copy(new.at[tile, :], out.at[tile, columns], sems.at[i])
+        )
         copies[-1].start()
     for copy in copies:
         copy.wait()
 
 
-def gram(own, held, passed, old):
-    height, length = old.shape
-    slab = 2 * own[0].shape[0]
-    return pl.pallas_call(
-        gram_kernel,
-        out_shape=struct(old.shape, F32),
-        in_specs=[VMEM] * 13,
+def gram(other, own, held, passed, old, begun=None):
+    height, length = 2 * old[0].shape[0], old[0].shape[1]
+    rows, width = own[0].shape
+    operands = (*own, *held, *passed, *map(in_vmem, old))
+    more = () if begun is None else (in_hbm(begun),)
+    return pl.pallas_call(
+        functools.partial(gram_kernel, other),
+        out_shape=struct((height, length), F32),
+        in_specs=[VMEM] * len(operands) + [ANY] * len(more),
         out_specs=ANY,
+        input_output_aliases={len(operands): 0} if more else {},
         scratch_shapes=[
-            pltpu.VMEM((slab, height), BF16),
-            pltpu.VMEM((slab, length), BF16),
-            pltpu.VMEM(old.shape, F32),
-            pltpu.SemaphoreType.DMA((height // TILE,)),
+            pltpu.VMEM((2 * rows, height), BF16),
+            pltpu.VMEM((2 * rows, width), BF16),
+            pltpu.VMEM((height, width), F32),
+            pltpu.SemaphoreType.DMA((height // GRAM_TILE,)),
         ],
-        compiler_params=params(24),
-        cost_estimate=cost(2 * slab * height * length, 8 * height * length),
+        compiler_params=params(16),
+        cost_estimate=cost(4 * rows * height * width, 8 * height * width),
         name="gram",
-    )(*own, *held, *passed, in_vmem(old))
-
-
-def after(value, other):
-    return lax.optimization_barrier((value, other))[0]
+    )(*operands, *more)
+
+
+def after(value, *others):
+    return lax.optimization_barrier((value, *others))[0]
 
 
 def square(stored, gram_old, w_enc, b_enc, b_dec):
-    b_dec, b_enc = b_dec[None, :], b_enc[None, :]
-
     beside = flip(stored, "row", 1)
     across = flip(stored, "row", 2)
-    out_a, x_a, w_out = first_send(stored, beside, b_dec, w_enc)
+    stored, b_dec, w_out = load_first(stored, b_dec[None, :], w_enc)
+    b_enc = b_enc[None, :]
+    out_a, x_a = send(stored, beside, b_dec, w_out)
+    shape = out_a.shape
+
+    def pair_sum(kept, sent):
+        return small(pair_kernel, "pair_sum", shape, kept, sent)
+
+    def codes(kept, sent, far):
+        return small(codes_kernel, "codes", shape, kept, sent, far, b_enc)
+
+    def choose(here, there):
+        return small(choose_kernel, "choose", shape, here, there)
+
     sent_a = flip(out_a, "col", 1)
     kept_a, w_keep = first_keep(x_a, w_enc)
     across = after(across, kept_a)
     slant = flip(across, "row", 1)
-    out_b, x_b = next_send(across, slant, b_dec, w_out)
-    shape = out_a.shape
-
-    def pair_sum(kept, sent):
-        return small(pair_kernel, "pair_sum", shape, kept, sent)
-
-    pair_a = pair_sum(kept_a, sent_a)
-    sent_b = flip(after(out_b, pair_a), "col", 1)
+    pair_a = pair_sum(kept_a, after(sent_a, across))
     far_a = flip(pair_a, "col", 2)
-    kept_b = next_keep(x_b, w_keep)
-    old = load(pair_a, gram_old)
-    pair_b = pair_sum(kept_b, sent_b)
-    far_b = flip(after(pair_b, old), "col", 2)
-
-    def finish(kept, sent, far):
-        own = small(codes_kernel, "codes", shape, kept, sent, far, b_enc)
-        other = flip(own, "col", 1)
-        own_x = flip(own, "row", 2)
-        other_x = flip(other, "row", 2)
-        held_own = small(choose_kernel, "choose", shape, own, own_x)
-        held_other = small(choose_kernel, "choose", shape, other, other_x)
-        return [own, other], [held_own, held_other]
-
-    far_a = after(far_a, old)
-    own_a, held_a = finish(kept_a, sent_a, far_a)
-    own_b, held_b = finish(kept_b, sent_b, far_b)
-    held = held_a + held_b
-    passed = [flip(piece, "row", 1) for piece in held]
-    return gram(own_a + own_b, held, passed, old)
+    out_b, x_b = send(across, after(slant, pair_a), b_dec, w_out)
+    sent_b = flip(out_b, "col", 1)
+    kept_b = keep(x_b, w_keep)
+    old_top = load_half(0, kept_b, gram_old)
+    far_a = after(far_a, old_top)
+    pair_b = pair_sum(kept_b, after(sent_b, far_a))
+    far_b = flip(pair_b, "col", 2)
+    own_a = codes(kept_a, sent_a, after(far_a, pair_b))
+    other_a, own_x_a = flip(own_a, "col", 1), flip(own_a, "row", 2)
+    old_bottom = load_half(1, own_a, gram_old)
+    far_b = after(far_b, old_bottom)
+    other_a, own_x_a = after(other_a, far_b), after(own_x_a, far_b)
+    own_b = codes(kept_b, sent_b, far_b)
+    other_b, own_x_b = flip(own_b, "col", 1), flip(own_b, "row", 2)
+    other_x_a, other_x_b = flip(other_a, "row", 2), flip(other_b, "row", 2)
+    rows = [own_a, other_a, own_b, other_b]
+    old = [old_top, old_bottom]
+    held_own = [choose(own_a, own_x_a), choose(own_b, own_x_b)]
+    begun = gram(0, rows, held_own, [flip(piece, "row", 1) for piece in held_own], old)
+    held_other = [choose(other_a, other_x_a), choose(other_b, after(other_x_b, begun))]
+    passed_other = [flip(piece, "row", 1) for piece in held_other]
+    return gram(1, rows, held_other, passed_other, old, begun)
 
 
 def shards(stored, gram_old, w_enc, b_enc, b_dec):

time: 54.1 us -> 47.8 us (0.88)
  waiting for transfers between devices: 17.7 us -> 9.25 us
  Pallas kernels: 19.2 us -> 22 us
  local copies, waits for them, and re-layouts: 1.64 us -> 0.01 us
  starting transfers between devices: 15.1 us -> 16.2 us
    ppermute x17, waiting for transfers between devices: 17.7 us -> 9.25 us  [flip(): return lax.ppermute(value, axis, [(i, i ^ bit) for i in range(4)])]
    pallas_call x5 -> x8, Pallas kernels: 16.5 us -> 19.2 us  [the longest x2 7.49 us: gram(): pl.pallas_call(functools.partial(gram_kernel, other), out_shape=struct((h...]
    unnamed x8 -> x2, local copies, waits for them, and re-layouts: 1.64 us -> 0.01 us
    ppermute x17, starting transfers between devices: 15.1 us -> 16.2 us  [flip(): return lax.ppermute(value, axis, [(i, i ^ bit) for i in range(4)])]
  transfers between devices with their start and end apart: 17 -> 17, of which waited for: 8 -> 7; matrix products, arithmetic and copies ran while one was open for 0% -> 0% of each run, Pallas kernels for 22% -> 34%
where the time goes in v3:
time: 47.8 us; the launch traced here: 47.7 us
  Pallas kernels  22 us (46%)
  starting transfers between devices  16.2 us (34%)
  waiting for transfers between devices  9.25 us (19%)
    ppermute x17, starting transfers between devices, flip(): return lax.ppermute(value, axis, [(i, i ^ bit) for i in range(4)])  16.2 us
    ppermute x17, waiting for transfers between devices, flip(): return lax.ppermute(value, axis, [(i, i ^ bit) for i in range(4)])  9.25 us
    pallas_call x2, Pallas kernels, gram(): pl.pallas_call(functools.partial(gram_kernel, other), out_shape=struct((h...  7.49 us
    pallas_call x2, Pallas kernels, load_half(): pl.pallas_call(functools.partial(load_kernel, part), out_shape=struct((ro...  6.79 us
    pallas_call x1, Pallas kernels, first_keep(): pl.pallas_call(first_keep_kernel, out_shape=(struct((rows, width), F32),...  2.5 us
    pallas_call x1, Pallas kernels, load_first(): pl.pallas_call(load_first_kernel, out_shape=(struct(stored.shape, BF16),...  2.31 us
    pallas_call x2, Pallas kernels, send(): pl.pallas_call(send_kernel, out_shape=(struct((rows, width), BF16), struc...  1.81 us
  transfers between devices with their start and end apart: 17, of which 7 were waited for; matrix products, arithmetic and copies ran while one was open for 0% of the time, Pallas kernels for 34%

profile of v3, /device:TPU:0, one launch (start us, length us, event | category | flops | bytes accessed | tf_op | source)
XLA Modules:
  0.0 47.7 jit_solution(9812199250750344020)
XLA Ops:
  0.5 2.5 %collective-permute-start.2 = (bf16[32,2048]{1,0:T(8,128)(2,1)}, bf16[32,2048]{1,0:T(8,128)(2,1)S(1)}, u32[]{:S(2)}, u32[]{:S(2)}) collective-permute-start(bf16[32,2048]{1,0:T(8,128)(2,1)} %stored.1), channel_id=1, source_target_pairs={{0,8},{4,12},{8,0},{12,4},{1,9},{5,13},{9,1},{13,5},{2,10},{6,14},... | collective-permute-start | bytes 393224 | tf_op jit(solution)/shard_map/ppermute | solution.py:43
  2.9 2.3 %load_first.1 = (bf16[32,2048]{1,0:T(8,128)(2,1)S(1)}, f32[1,2048]{1,0:T(1,128)S(1)}, bf16[2048,1024]{1,0:T(8,128)(2,1)S(1)}) custom-call(bf16[32,2048]{1,0:T(8,128)(2,1)} %stored.1, f32[1,2048]{1,0:T(1,128)} %bitcast.4, bf16[2048,2048]{1,0:T(8,128)(2,1)} %w.3), custom_call_target="tpu_custom_call" | custom-call | bytes 4194304 | tf_op jit(solution)/shard_map/load_first/pallas_call | solution.py:125
  5.3 0.9 %send.2 = (bf16[64,1024]{1,0:T(8,128)(2,1)S(1)}, bf16[64,2048]{1,0:T(8,128)(2,1)S(1)}) custom-call(bf16[32,2048]{1,0:T(8,128)(2,1)S(1)} %get-tuple-element.24.here, bf16[32,2048]{1,0:T(8,128)(2,1)S(1)} %collective-permute-done.beside, f32[1,2048]{1,0:T(1,128)S(1)} %get-tuple-element.25.b_dec, bf16[2048,1024]{1,0:T(8,128)(2,1)S(1)} %get-tuple-element.26.held), custom_call_target="tpu_custom_call" | custom-call | flops 268435456 | bytes 262144 | tf_op jit(solution)/shard_map/send/pallas_call | solution.py:172
  6.2 1.6 %collective-permute-start.1 = (bf16[64,1024]{1,0:T(8,128)(2,1)S(1)}, bf16[64,1024]{1,0:T(8,128)(2,1)S(1)}, u32[]{:S(2)}, u32[]{:S(2)}) collective-permute-start(bf16[64,1024]{1,0:T(8,128)(2,1)S(1)} %get-tuple-element.29), channel_id=1, source_target_pairs={{0,1},{1,0},{2,3},{3,2},{4,5},{5,4},{6,7},{7,6},{8,9},{9,8},{10,11... | collective-permute-start | bytes 393224 | tf_op jit(solution)/shard_map/ppermute | solution.py:43
  7.8 2.5 %first_keep.1 = (f32[64,1024]{1,0:T(8,128)S(1)}, bf16[2048,1024]{1,0:T(8,128)(2,1)S(1)}) custom-call(bf16[64,2048]{1,0:T(8,128)(2,1)S(1)} %get-tuple-element.27.x, bf16[2048,2048]{1,0:T(8,128)(2,1)} %w.3), custom_call_target="tpu_custom_call" | custom-call | flops 268435456 | bytes 4194304 | tf_op jit(solution)/shard_map/first_keep/pallas_call | solution.py:146
  10.4 1.5 %collective-permute-done.1.sent = bf16[64,1024]{1,0:T(8,128)(2,1)S(1)} collective-permute-done((bf16[64,1024]{1,0:T(8,128)(2,1)S(1)}, bf16[64,1024]{1,0:T(8,128)(2,1)S(1)}, u32[]{:S(2)}, u32[]{:S(2)}) %collective-permute-start.1) | collective-permute-done | bytes 131104 | tf_op jit(solution)/shard_map/ppermute | solution.py:43
  11.9 2.7 %collective-permute-start.3 = (bf16[64,1024]{1,0:T(8,128)(2,1)S(1)}, bf16[64,1024]{1,0:T(8,128)(2,1)S(1)}, u32[]{:S(2)}, u32[]{:S(2)}) collective-permute-start(bf16[64,1024]{1,0:T(8,128)(2,1)S(1)} %pair_sum.2), channel_id=1, source_target_pairs={{0,2},{1,3},{2,0},{3,1},{4,6},{5,7},{6,4},{7,5},{8,10},{9,11},{10,... | collective-permute-start | bytes 393224 | tf_op jit(solution)/shard_map/ppermute | solution.py:43
  14.6 0.9 %send.3 = (bf16[64,1024]{1,0:T(8,128)(2,1)S(1)}, bf16[64,2048]{1,0:T(8,128)(2,1)S(1)}) custom-call(bf16[32,2048]{1,0:T(8,128)(2,1)S(1)} %collective-permute-done.2.here, bf16[32,2048]{1,0:T(8,128)(2,1)S(1)} %collective-permute-done.4.beside, f32[1,2048]{1,0:T(1,128)S(1)} %get-tuple-element.25.b_dec, bf16[2048,1024]{1,0:T(8,128)(2,1)S(1)} %get-tuple-element.26.held), custom_call_target="tpu_custom_call" | custom-call | flops 268435456 | bytes 262144 | tf_op jit(solution)/shard_map/send/pallas_call | solution.py:172
  15.5 1.6 %collective-permute-start.5 = (bf16[64,1024]{1,0:T(8,128)(2,1)S(1)}, bf16[64,1024]{1,0:T(8,128)(2,1)S(1)}, u32[]{:S(2)}, u32[]{:S(2)}) collective-permute-start(bf16[64,1024]{1,0:T(8,128)(2,1)S(1)} %get-tuple-element.36), channel_id=1, source_target_pairs={{0,1},{1,0},{2,3},{3,2},{4,5},{5,4},{6,7},{7,6},{8,9},{9,8},{10,11... | collective-permute-start | bytes 393224 | tf_op jit(solution)/shard_map/ppermute | solution.py:43
  17.1 0.8 %keep.1._.kept = f32[64,1024]{1,0:T(8,128)S(1)} custom-call(bf16[64,2048]{1,0:T(8,128)(2,1)S(1)} %get-tuple-element.33.x, bf16[2048,1024]{1,0:T(8,128)(2,1)S(1)} %get-tuple-element.34.held), custom_call_target="tpu_custom_call" | custom-call | flops 268435456 | bytes 262144 | tf_op jit(solution)/shard_map/keep/pallas_call | solution.py:185
  18.0 3.4 %load_half.2.refs_8_ = f32[1024,2048]{1,0:T(8,128)S(1)} custom-call(f32[64,1024]{1,0:T(8,128)S(1)} %keep.1._.kept, f32[2048,2048]{1,0:T(8,128)} %source.3), custom_call_target="tpu_custom_call" | custom-call | bytes 33554432 | tf_op jit(solution)/shard_map/load_half/pallas_call | solution.py:239
  21.8 0.9 %collective-permute-start.7 = (bf16[64,1024]{1,0:T(8,128)(2,1)S(1)}, bf16[64,1024]{1,0:T(8,128)(2,1)S(1)}, u32[]{:S(2)}, u32[]{:S(2)}) collective-permute-start(bf16[64,1024]{1,0:T(8,128)(2,1)S(1)} %pair_sum.3), channel_id=1, source_target_pairs={{0,2},{1,3},{2,0},{3,1},{4,6},{5,7},{6,4},{7,5},{8,10},{9,11},{10,... | collective-permute-start | bytes 393224 | tf_op jit(solution)/shard_map/ppermute | solution.py:43
  22.8 0.6 %collective-permute-start.11 = (bf16[64,1024]{1,0:T(8,128)(2,1)S(1)}, bf16[64,1024]{1,0:T(8,128)(2,1)S(1)}, u32[]{:S(2)}, u32[]{:S(2)}) collective-permute-start(bf16[64,1024]{1,0:T(8,128)(2,1)S(1)} %codes.2._.here.refs_0_), channel_id=1, source_target_pairs={{0,8},{4,12},{8,0},{12,4},{1,9},{5,13},{9,1},{13,5},{2,10},{6,14},... | collective-permute-start | bytes 393224 | tf_op jit(solution)/shard_map/ppermute | solution.py:43
  23.4 2.4 %collective-permute-start.6 = (bf16[64,1024]{1,0:T(8,128)(2,1)S(1)}, bf16[64,1024]{1,0:T(8,128)(2,1)S(1)}, u32[]{:S(2)}, u32[]{:S(2)}) collective-permute-start(bf16[64,1024]{1,0:T(8,128)(2,1)S(1)} %codes.2._.here.refs_0_), channel_id=1, source_target_pairs={{0,1},{1,0},{2,3},{3,2},{4,5},{5,4},{6,7},{7,6},{8,9},{9,8},{10,11... | collective-permute-start | bytes 393224 | tf_op jit(solution)/shard_map/ppermute | solution.py:43
  25.8 3.4 %load_half.3.refs_9_ = f32[1024,2048]{1,0:T(8,128)S(1)} custom-call(bf16[64,1024]{1,0:T(8,128)(2,1)S(1)} %codes.2._.here.refs_0_, f32[2048,2048]{1,0:T(8,128)} %source.3), custom_call_target="tpu_custom_call" | custom-call | bytes 33554432 | tf_op jit(solution)/shard_map/load_half/pallas_call | solution.py:239
  29.2 0.9 %collective-permute-done.7.far = bf16[64,1024]{1,0:T(8,128)(2,1)S(1)} collective-permute-done((bf16[64,1024]{1,0:T(8,128)(2,1)S(1)}, bf16[64,1024]{1,0:T(8,128)(2,1)S(1)}, u32[]{:S(2)}, u32[]{:S(2)}) %collective-permute-start.7) | collective-permute-done | bytes 131104 | tf_op jit(solution)/shard_map/ppermute | solution.py:43
  30.2 0.7 %collective-permute-start.12 = (bf16[64,1024]{1,0:T(8,128)(2,1)S(1)}, bf16[64,1024]{1,0:T(8,128)(2,1)S(1)}, u32[]{:S(2)}, u32[]{:S(2)}) collective-permute-start(bf16[64,1024]{1,0:T(8,128)(2,1)S(1)} %codes.3.here.refs_2_), channel_id=1, source_target_pairs={{0,8},{4,12},{8,0},{12,4},{1,9},{5,13},{9,1},{13,5},{2,10},{6,14},... | collective-permute-start | bytes 393224 | tf_op jit(solution)/shard_map/ppermute | solution.py:43
  31.0 1.4 %collective-permute-start.9 = (bf16[64,1024]{1,0:T(8,128)(2,1)S(1)}, bf16[64,1024]{1,0:T(8,128)(2,1)S(1)}, u32[]{:S(2)}, u32[]{:S(2)}) collective-permute-start(bf16[64,1024]{1,0:T(8,128)(2,1)S(1)} %collective-permute-done.6.here.refs_1_), channel_id=1, source_target_pairs={{0,8},{4,12},{8,0},{12,4},{1,9},{5,13},{9,1},{13,5},{2,10},{6,14},... | collective-permute-start | bytes 393224 | tf_op jit(solution)/shard_map/ppermute | solution.py:43
  32.4 4.1 %collective-permute-done.12.there = bf16[64,1024]{1,0:T(8,128)(2,1)S(1)} collective-permute-done((bf16[64,1024]{1,0:T(8,128)(2,1)S(1)}, bf16[64,1024]{1,0:T(8,128)(2,1)S(1)}, u32[]{:S(2)}, u32[]{:S(2)}) %collective-permute-start.12) | collective-permute-done | bytes 131104 | tf_op jit(solution)/shard_map/ppermute | solution.py:43
  36.6 0.9 %collective-permute-start.10 = (bf16[64,1024]{1,0:T(8,128)(2,1)S(1)}, bf16[64,1024]{1,0:T(8,128)(2,1)S(1)}, u32[]{:S(2)}, u32[]{:S(2)}) collective-permute-start(bf16[64,1024]{1,0:T(8,128)(2,1)S(1)} %collective-permute-done.8.refs_3_.here), channel_id=1, source_target_pairs={{0,8},{4,12},{8,0},{12,4},{1,9},{5,13},{9,1},{13,5},{2,10},{6,14},... | collective-permute-start | bytes 393224 | tf_op jit(solution)/shard_map/ppermute | solution.py:43
  38.0 3.8 %gram.2.refs_10_ = f32[2048,2048]{1,0:T(8,128)} custom-call(bf16[64,1024]{1,0:T(8,128)(2,1)S(1)} %codes.2._.here.refs_0_, bf16[64,1024]{1,0:T(8,128)(2,1)S(1)} %collective-permute-done.6.here.refs_1_, bf16[64,1024]{1,0:T(8,128)(2,1)S(1)} %codes.3.here.refs_2_, bf16[64,1024]{1,0:T(8,128)(2,1)S(1)} %collective-permute-done.8.refs_3_.here, ...), custom_call_target="tpu_custom_call" | custom-call | flops 536870912 | bytes 16777216 | tf_op jit(solution)/shard_map/gram/pallas_call | solution.py:295
  41.7 0.7 %collective-permute-done.10.there = bf16[64,1024]{1,0:T(8,128)(2,1)S(1)} collective-permute-done((bf16[64,1024]{1,0:T(8,128)(2,1)S(1)}, bf16[64,1024]{1,0:T(8,128)(2,1)S(1)}, u32[]{:S(2)}, u32[]{:S(2)}) %collective-permute-start.10) | collective-permute-done | bytes 131104 | tf_op jit(solution)/shard_map/ppermute | solution.py:43
  42.6 1.3 %collective-permute-done.16.refs_7_ = bf16[64,1024]{1,0:T(8,128)(2,1)S(1)} collective-permute-done((bf16[64,1024]{1,0:T(8,128)(2,1)S(1)}, bf16[64,1024]{1,0:T(8,128)(2,1)S(1)}, u32[]{:S(2)}, u32[]{:S(2)}) %collective-permute-start.16) | collective-permute-done | bytes 131104 | tf_op jit(solution)/shard_map/ppermute | solution.py:43
  43.9 3.7 %gram.3 = f32[2048,2048]{1,0:T(8,128)} custom-call(bf16[64,1024]{1,0:T(8,128)(2,1)S(1)} %codes.2._.here.refs_0_, bf16[64,1024]{1,0:T(8,128)(2,1)S(1)} %collective-permute-done.6.here.refs_1_, bf16[64,1024]{1,0:T(8,128)(2,1)S(1)} %codes.3.here.refs_2_, bf16[64,1024]{1,0:T(8,128)(2,1)S(1)} %collective-permute-done.8.refs_3_.here, ...), custom_call_target="tpu_custom_call", output_to_operand_aliasing={{}: (10, {})} | custom-call | flops 536870912 | bytes 16777216 | tf_op jit(solution)/shard_map/gram/pallas_call | solution.py:295
  (29 shorter events, 1.7 us)
Async XLA Ops:
  0.0 5.3 %collective-permute-start = (bf16[32,2048]{1,0:T(8,128)(2,1)}, bf16[32,2048]{1,0:T(8,128)(2,1)S(1)}, u32[]{:S(2)}, u32[]{:S(2)}) collective-permute-start(bf16[32,2048]{1,0:T(8,128)(2,1)} %stored.1), channel_id=1, source_target_pairs={{0,4},{4,0},{8,12},{12,8},{1,5},{5,1},{9,13},{13,9},{2,6},{6,2},{1... | collective-permute-start | bytes 393224 | tf_op jit(solution)/shard_map/ppermute | solution.py:43
  0.5 9.9 %collective-permute-start.2 = (bf16[32,2048]{1,0:T(8,128)(2,1)}, bf16[32,2048]{1,0:T(8,128)(2,1)S(1)}, u32[]{:S(2)}, u32[]{:S(2)}) collective-permute-start(bf16[32,2048]{1,0:T(8,128)(2,1)} %stored.1), channel_id=1, source_target_pairs={{0,8},{4,12},{8,0},{12,4},{1,9},{5,13},{9,1},{13,5},{2,10},{6,14},... | collective-permute-start | bytes 393224 | tf_op jit(solution)/shard_map/ppermute | solution.py:43
  6.2 5.7 %collective-permute-start.1 = (bf16[64,1024]{1,0:T(8,128)(2,1)S(1)}, bf16[64,1024]{1,0:T(8,128)(2,1)S(1)}, u32[]{:S(2)}, u32[]{:S(2)}) collective-permute-start(bf16[64,1024]{1,0:T(8,128)(2,1)S(1)} %get-tuple-element.29), channel_id=1, source_target_pairs={{0,1},{1,0},{2,3},{3,2},{4,5},{5,4},{6,7},{7,6},{8,9},{9,8},{10,11... | collective-permute-start | bytes 393224 | tf_op jit(solution)/shard_map/ppermute | solution.py:43
  10.4 4.2 %collective-permute-start.4 = (bf16[32,2048]{1,0:T(8,128)(2,1)S(1)}, bf16[32,2048]{1,0:T(8,128)(2,1)S(1)}, u32[]{:S(2)}, u32[]{:S(2)}) collective-permute-start(bf16[32,2048]{1,0:T(8,128)(2,1)S(1)} %collective-permute-done.2.here), channel_id=1, source_target_pairs={{0,4},{4,0},{8,12},{12,8},{1,5},{5,1},{9,13},{13,9},{2,6},{6,2},{1... | collective-permute-start | bytes 393224 | tf_op jit(solution)/shard_map/ppermute | solution.py:43
  11.9 9.5 %collective-permute-start.3 = (bf16[64,1024]{1,0:T(8,128)(2,1)S(1)}, bf16[64,1024]{1,0:T(8,128)(2,1)S(1)}, u32[]{:S(2)}, u32[]{:S(2)}) collective-permute-start(bf16[64,1024]{1,0:T(8,128)(2,1)S(1)} %pair_sum.2), channel_id=1, source_target_pairs={{0,2},{1,3},{2,0},{3,1},{4,6},{5,7},{6,4},{7,5},{8,10},{9,11},{10,... | collective-permute-start | bytes 393224 | tf_op jit(solution)/shard_map/ppermute | solution.py:43
  15.5 6.3 %collective-permute-start.5 = (bf16[64,1024]{1,0:T(8,128)(2,1)S(1)}, bf16[64,1024]{1,0:T(8,128)(2,1)S(1)}, u32[]{:S(2)}, u32[]{:S(2)}) collective-permute-start(bf16[64,1024]{1,0:T(8,128)(2,1)S(1)} %get-tuple-element.36), channel_id=1, source_target_pairs={{0,1},{1,0},{2,3},{3,2},{4,5},{5,4},{6,7},{7,6},{8,9},{9,8},{10,11... | collective-permute-start | bytes 393224 | tf_op jit(solution)/shard_map/ppermute | solution.py:43
  18.0 4.8 %copy-start = (f32[2048]{0:T(1024)S(1)}, f32[2048]{0:T(1024)}, u32[]{:S(2)}) copy-start(f32[2048]{0:T(1024)} %param.8) | copy-start | bytes 24580
  21.8 8.3 %collective-permute-start.7 = (bf16[64,1024]{1,0:T(8,128)(2,1)S(1)}, bf16[64,1024]{1,0:T(8,128)(2,1)S(1)}, u32[]{:S(2)}, u32[]{:S(2)}) collective-permute-start(bf16[64,1024]{1,0:T(8,128)(2,1)S(1)} %pair_sum.3), channel_id=1, source_target_pairs={{0,2},{1,3},{2,0},{3,1},{4,6},{5,7},{6,4},{7,5},{8,10},{9,11},{10,... | collective-permute-start | bytes 393224 | tf_op jit(solution)/shard_map/ppermute | solution.py:43
  22.8 8.2 %collective-permute-start.11 = (bf16[64,1024]{1,0:T(8,128)(2,1)S(1)}, bf16[64,1024]{1,0:T(8,128)(2,1)S(1)}, u32[]{:S(2)}, u32[]{:S(2)}) collective-permute-start(bf16[64,1024]{1,0:T(8,128)(2,1)S(1)} %codes.2._.here.refs_0_), channel_id=1, source_target_pairs={{0,8},{4,12},{8,0},{12,4},{1,9},{5,13},{9,1},{13,5},{2,10},{6,14},... | collective-permute-start | bytes 393224 | tf_op jit(solution)/shard_map/ppermute | solution.py:43
  23.4 7.6 %collective-permute-start.6 = (bf16[64,1024]{1,0:T(8,128)(2,1)S(1)}, bf16[64,1024]{1,0:T(8,128)(2,1)S(1)}, u32[]{:S(2)}, u32[]{:S(2)}) collective-permute-start(bf16[64,1024]{1,0:T(8,128)(2,1)S(1)} %codes.2._.here.refs_0_), channel_id=1, source_target_pairs={{0,1},{1,0},{2,3},{3,2},{4,5},{5,4},{6,7},{7,6},{8,9},{9,8},{10,11... | collective-permute-start | bytes 393224 | tf_op jit(solution)/shard_map/ppermute | solution.py:43
  30.2 6.2 %collective-permute-start.12 = (bf16[64,1024]{1,0:T(8,128)(2,1)S(1)}, bf16[64,1024]{1,0:T(8,128)(2,1)S(1)}, u32[]{:S(2)}, u32[]{:S(2)}) collective-permute-start(bf16[64,1024]{1,0:T(8,128)(2,1)S(1)} %codes.3.here.refs_2_), channel_id=1, source_target_pairs={{0,8},{4,12},{8,0},{12,4},{1,9},{5,13},{9,1},{13,5},{2,10},{6,14},... | collective-permute-start | bytes 393224 | tf_op jit(solution)/shard_map/ppermute | solution.py:43
  31.0 5.6 %collective-permute-start.8 = (bf16[64,1024]{1,0:T(8,128)(2,1)S(1)}, bf16[64,1024]{1,0:T(8,128)(2,1)S(1)}, u32[]{:S(2)}, u32[]{:S(2)}) collective-permute-start(bf16[64,1024]{1,0:T(8,128)(2,1)S(1)} %codes.3.here.refs_2_), channel_id=1, source_target_pairs={{0,1},{1,0},{2,3},{3,2},{4,5},{5,4},{6,7},{7,6},{8,9},{9,8},{10,11... | collective-permute-start | bytes 393224 | tf_op jit(solution)/shard_map/ppermute | solution.py:43
  31.0 6.9 %collective-permute-start.9 = (bf16[64,1024]{1,0:T(8,128)(2,1)S(1)}, bf16[64,1024]{1,0:T(8,128)(2,1)S(1)}, u32[]{:S(2)}, u32[]{:S(2)}) collective-permute-start(bf16[64,1024]{1,0:T(8,128)(2,1)S(1)} %collective-permute-done.6.here.refs_1_), channel_id=1, source_target_pairs={{0,8},{4,12},{8,0},{12,4},{1,9},{5,13},{9,1},{13,5},{2,10},{6,14},... | collective-permute-start | bytes 393224 | tf_op jit(solution)/shard_map/ppermute | solution.py:43
  32.4 5.6 %collective-permute-start.13 = (bf16[64,1024]{1,0:T(8,128)(2,1)S(1)}, bf16[64,1024]{1,0:T(8,128)(2,1)S(1)}, u32[]{:S(2)}, u32[]{:S(2)}) collective-permute-start(bf16[64,1024]{1,0:T(8,128)(2,1)S(1)} %choose.5.refs_4_), channel_id=1, source_target_pairs={{0,4},{4,0},{8,12},{12,8},{1,5},{5,1},{9,13},{13,9},{2,6},{6,2},{1... | collective-permute-start | bytes 393224 | tf_op jit(solution)/shard_map/ppermute | solution.py:43
  36.5 1.5 %collective-permute-start.14 = (bf16[64,1024]{1,0:T(8,128)(2,1)S(1)}, bf16[64,1024]{1,0:T(8,128)(2,1)S(1)}, u32[]{:S(2)}, u32[]{:S(2)}) collective-permute-start(bf16[64,1024]{1,0:T(8,128)(2,1)S(1)} %choose.6.refs_5_), channel_id=1, source_target_pairs={{0,4},{4,0},{8,12},{12,8},{1,5},{5,1},{9,13},{13,9},{2,6},{6,2},{1... | collective-permute-start | bytes 393224 | tf_op jit(solution)/shard_map/ppermute | solution.py:43
  36.6 5.9 %collective-permute-start.10 = (bf16[64,1024]{1,0:T(8,128)(2,1)S(1)}, bf16[64,1024]{1,0:T(8,128)(2,1)S(1)}, u32[]{:S(2)}, u32[]{:S(2)}) collective-permute-start(bf16[64,1024]{1,0:T(8,128)(2,1)S(1)} %collective-permute-done.8.refs_3_.here), channel_id=1, source_target_pairs={{0,8},{4,12},{8,0},{12,4},{1,9},{5,13},{9,1},{13,5},{2,10},{6,14},... | collective-permute-start | bytes 393224 | tf_op jit(solution)/shard_map/ppermute | solution.py:43
  37.9 4.7 %collective-permute-start.15 = (bf16[64,1024]{1,0:T(8,128)(2,1)S(1)}, bf16[64,1024]{1,0:T(8,128)(2,1)S(1)}, u32[]{:S(2)}, u32[]{:S(2)}) collective-permute-start(bf16[64,1024]{1,0:T(8,128)(2,1)S(1)} %choose.4.refs_4_), channel_id=1, source_target_pairs={{0,4},{4,0},{8,12},{12,8},{1,5},{5,1},{9,13},{13,9},{2,6},{6,2},{1... | collective-permute-start | bytes 393224 | tf_op jit(solution)/shard_map/ppermute | solution.py:43
  42.5 1.4 %collective-permute-start.16 = (bf16[64,1024]{1,0:T(8,128)(2,1)S(1)}, bf16[64,1024]{1,0:T(8,128)(2,1)S(1)}, u32[]{:S(2)}, u32[]{:S(2)}) collective-permute-start(bf16[64,1024]{1,0:T(8,128)(2,1)S(1)} %choose.7.refs_5_), channel_id=1, source_target_pairs={{0,4},{4,0},{8,12},{12,8},{1,5},{5,1},{9,13},{13,9},{2,6},{6,2},{1... | collective-permute-start | bytes 393224 | tf_op jit(solution)/shard_map/ppermute | solution.py:43

commit v4 on v3

--- a/solution.py
+++ b/solution.py
@@ -227,6 +227,34 @@
         out[...] = there[...]
 
 
+def pick_kernel(here, there, out):
+    row, col = row_and_col()
+    home = (row >> 1) == (col >> 1)
+
+    @pl.when(home)
+    def _():
+        out[...] = here[...]
+
+    @pl.when(jnp.logical_not(home))
+    def _():
+        out[...] = there[...]
+
+
+def same_parity():
+    row, col = row_and_col()
+    return ((row ^ col) & 1) == 0
+
+
+def next_kernel(picked, passed, out):
+    @pl.when(same_parity())
+    def _():
+        out[...] = passed[...]
+
+    @pl.when(jnp.logical_not(same_parity()))
+    def _():
+        out[...] = picked[...]
+
+
 def load_kernel(part, _, source, out, sem):
     rows = out.shape[0]
     copy = pltpu.make_async_copy(source.at[pl.ds(part * rows, rows), :], out, sem)
@@ -249,10 +277,11 @@
 
 
 def gram_kernel(other, *refs):
-    pieces, olds, (out, left, right, new, sems) = refs[:8], refs[8:10], refs[-5:]
+    pieces, columns, olds = refs[:4], refs[4 : 8 - other], refs[8 - other : 10 - other]
+    out, left, right, new, sems = refs[-5:]
     rows, width = pieces[0].shape
     row, col = row_and_col()
-    held = (row == col) | ((row ^ 2) == col)
+    here = ((row == col) | ((row ^ 2) == col), same_parity())
     for k in range(4):
         chunk = k // 2
         half = window(((col & 1) ^ (k % 2)) * width, width)
@@ -260,16 +289,20 @@
     for chunk in range(2):
         place = window(((col >> 1) ^ chunk) * rows, rows)
 
-        @pl.when(held)
+        if other and chunk == 1:
+            right[place, :] = columns[1][...]
+            continue
+
+        @pl.when(here[chunk])
         def _():
-            right[place, :] = pieces[4 + chunk][...]
-
-        @pl.when(jnp.logical_not(held))
+            right[place, :] = columns[chunk][...]
+
+        @pl.when(jnp.logical_not(here[chunk]))
         def _():
-            right[place, :] = pieces[6 + chunk][...]
+            right[place, :] = columns[2 + chunk][...]
 
     scale = 1.0 / left.shape[0]
-    columns = window(((col & 1) ^ other) * width, width)
+    span = window(((col & 1) ^ other) * width, width)
     copies = []
     tiles = out.shape[0] // GRAM_TILE
     for i in range(tiles):
@@ -278,19 +311,19 @@
         product = lax.dot_general(
             left[:, tile], right[...], (((0,), (0,)), ((), ())), preferred_element_type=F32
         )
-        new[tile, :] = old[place, columns] + product * scale
+        new[tile, :] = old[place, span] + product * scale
         copies.append(
-            pltpu.make_async_copy(new.at[tile, :], out.at[tile, columns], sems.at[i])
+            pltpu.make_async_copy(new.at[tile, :], out.at[tile, span], sems.at[i])
         )
         copies[-1].start()
     for copy in copies:
         copy.wait()
 
 
-def gram(other, own, held, passed, old, begun=None):
+def gram(other, own, columns, old, begun=None):
     height, length = 2 * old[0].shape[0], old[0].shape[1]
     rows, width = own[0].shape
-    operands = (*own, *held, *passed, *map(in_vmem, old))
+    operands = (*own, *columns, *map(in_vmem, old))
     more = () if begun is None else (in_hbm(begun),)
     return pl.pallas_call(
         functools.partial(gram_kernel, other),
@@ -330,6 +363,12 @@
 
     def choose(here, there):
         return small(choose_kernel, "choose", shape, here, there)
+
+    def pick(here, there):
+        return small(pick_kernel, "pick", shape, here, there)
+
+    def next_column(picked, passed):
+        return small(next_kernel, "next_column", shape, picked, passed)
 
     sent_a = flip(out_a, "col", 1)
     kept_a, w_keep = first_keep(x_a, w_enc)
@@ -347,18 +386,24 @@
     own_a = codes(kept_a, sent_a, after(far_a, pair_b))
     other_a, own_x_a = flip(own_a, "col", 1), flip(own_a, "row", 2)
     old_bottom = load_half(1, own_a, gram_old)
-    far_b = after(far_b, old_bottom)
-    other_a, own_x_a = after(other_a, far_b), after(own_x_a, far_b)
-    own_b = codes(kept_b, sent_b, far_b)
+    own_x_a = after(own_x_a, old_bottom)
+    other_x_a = flip(own_x_a, "col", 1)
+    far_b = after(far_b, old_bottom, own_x_a)
+    other_a = after(other_a, far_b)
+    own_b = codes(kept_b, sent_b, after(far_b, other_a))
     other_b, own_x_b = flip(own_b, "col", 1), flip(own_b, "row", 2)
-    other_x_a, other_x_b = flip(other_a, "row", 2), flip(other_b, "row", 2)
+    held_own_a = choose(own_a, own_x_a)
+    passed_own_a = flip(held_own_a, "row", 1)
+    held_other_a = choose(other_a, after(other_x_a, own_b))
+    passed_other_a = flip(held_other_a, "row", 1)
+    pick_b = pick(own_b, after(own_x_b, held_other_a))
+    passed_b = after(flip(pick_b, "row", 1), other_b, passed_own_a, passed_other_a)
+    column_b = flip(next_column(pick_b, passed_b), "col", 1)
     rows = [own_a, other_a, own_b, other_b]
     old = [old_top, old_bottom]
-    held_own = [choose(own_a, own_x_a), choose(own_b, own_x_b)]
-    begun = gram(0, rows, held_own, [flip(piece, "row", 1) for piece in held_own], old)
-    held_other = [choose(other_a, other_x_a), choose(other_b, after(other_x_b, begun))]
-    passed_other = [flip(piece, "row", 1) for piece in held_other]
-    return gram(1, rows, held_other, passed_other, old, begun)
+    begun = gram(0, rows, [held_own_a, pick_b, passed_own_a, passed_b], old)
+    columns = [held_other_a, after(column_b, begun), passed_other_a]
+    return gram(1, rows, columns, old, begun)
 
 
 def shards(stored, gram_old, w_enc, b_enc, b_dec):

time: 47.8 us -> 47.2 us (0.987)
  waiting for transfers between devices: 9.25 us -> 8.38 us
    ppermute x17 -> x16, waiting for transfers between devices: 9.25 us -> 8.38 us  [flip(): return lax.ppermute(value, axis, [(i, i ^ bit) for i in range(4)])]
    ppermute x17 -> x16, starting transfers between devices: 16.2 us -> 16.5 us  [flip(): return lax.ppermute(value, axis, [(i, i ^ bit) for i in range(4)])]
  transfers between devices with their start and end apart: 17 -> 16, of which waited for: 7 -> 9; matrix products, arithmetic and copies ran while one was open for 0% -> 0% of each run, Pallas kernels for 34% -> 35%
where the time goes in v4:
time: 47.2 us; the launch traced here: 47 us
  Pallas kernels  21.9 us (46%)
  starting transfers between devices  16.5 us (35%)
  waiting for transfers between devices  8.38 us (18%)
    ppermute x16, starting transfers between devices, flip(): return lax.ppermute(value, axis, [(i, i ^ bit) for i in range(4)])  16.5 us
    ppermute x16, waiting for transfers between devices, flip(): return lax.ppermute(value, axis, [(i, i ^ bit) for i in range(4)])  8.38 us
    pallas_call x2, Pallas kernels, gram(): pl.pallas_call(functools.partial(gram_kernel, other), out_shape=struct((h...  7.47 us
    pallas_call x2, Pallas kernels, load_half(): pl.pallas_call(functools.partial(load_kernel, part), out_shape=struct((ro...  6.79 us
    pallas_call x1, Pallas kernels, first_keep(): pl.pallas_call(first_keep_kernel, out_shape=(struct((rows, width), F32),...  2.5 us
    pallas_call x1, Pallas kernels, load_first(): pl.pallas_call(load_first_kernel, out_shape=(struct(stored.shape, BF16),...  2.31 us
    pallas_call x2, Pallas kernels, send(): pl.pallas_call(send_kernel, out_shape=(struct((rows, width), BF16), struc...  1.82 us
  transfers between devices with their start and end apart: 16, of which 9 were waited for; matrix products, arithmetic and copies ran while one was open for 0% of the time, Pallas kernels for 35%

profile of v4, /device:TPU:0, one launch (start us, length us, event | category | flops | bytes accessed | tf_op | source)
XLA Modules:
  0.0 47.0 jit_solution(15152653534975293566)
XLA Ops:
  0.5 2.5 %collective-permute-start.2 = (bf16[32,2048]{1,0:T(8,128)(2,1)}, bf16[32,2048]{1,0:T(8,128)(2,1)S(1)}, u32[]{:S(2)}, u32[]{:S(2)}) collective-permute-start(bf16[32,2048]{1,0:T(8,128)(2,1)} %stored.1), channel_id=1, source_target_pairs={{0,8},{4,12},{8,0},{12,4},{1,9},{5,13},{9,1},{13,5},{2,10},{6,14},... | collective-permute-start | bytes 393224 | tf_op jit(solution)/shard_map/ppermute | solution.py:43
  2.9 2.3 %load_first.1 = (bf16[32,2048]{1,0:T(8,128)(2,1)S(1)}, f32[1,2048]{1,0:T(1,128)S(1)}, bf16[2048,1024]{1,0:T(8,128)(2,1)S(1)}) custom-call(bf16[32,2048]{1,0:T(8,128)(2,1)} %stored.1, f32[1,2048]{1,0:T(1,128)} %bitcast.4, bf16[2048,2048]{1,0:T(8,128)(2,1)} %w.3), custom_call_target="tpu_custom_call" | custom-call | bytes 4194304 | tf_op jit(solution)/shard_map/load_first/pallas_call | solution.py:125
  5.3 0.9 %send.2 = (bf16[64,1024]{1,0:T(8,128)(2,1)S(1)}, bf16[64,2048]{1,0:T(8,128)(2,1)S(1)}) custom-call(bf16[32,2048]{1,0:T(8,128)(2,1)S(1)} %get-tuple-element.28.here, bf16[32,2048]{1,0:T(8,128)(2,1)S(1)} %collective-permute-done.beside, f32[1,2048]{1,0:T(1,128)S(1)} %get-tuple-element.29.b_dec, bf16[2048,1024]{1,0:T(8,128)(2,1)S(1)} %get-tuple-element.30.held), custom_call_target="tpu_custom_call" | custom-call | flops 268435456 | bytes 262144 | tf_op jit(solution)/shard_map/send/pallas_call | solution.py:172
  6.2 1.6 %collective-permute-start.1 = (bf16[64,1024]{1,0:T(8,128)(2,1)S(1)}, bf16[64,1024]{1,0:T(8,128)(2,1)S(1)}, u32[]{:S(2)}, u32[]{:S(2)}) collective-permute-start(bf16[64,1024]{1,0:T(8,128)(2,1)S(1)} %get-tuple-element.33), channel_id=1, source_target_pairs={{0,1},{1,0},{2,3},{3,2},{4,5},{5,4},{6,7},{7,6},{8,9},{9,8},{10,11... | collective-permute-start | bytes 393224 | tf_op jit(solution)/shard_map/ppermute | solution.py:43
  7.8 2.5 %first_keep.1 = (f32[64,1024]{1,0:T(8,128)S(1)}, bf16[2048,1024]{1,0:T(8,128)(2,1)S(1)}) custom-call(bf16[64,2048]{1,0:T(8,128)(2,1)S(1)} %get-tuple-element.31.x, bf16[2048,2048]{1,0:T(8,128)(2,1)} %w.3), custom_call_target="tpu_custom_call" | custom-call | flops 268435456 | bytes 4194304 | tf_op jit(solution)/shard_map/first_keep/pallas_call | solution.py:146
  10.4 1.5 %collective-permute-done.1.sent = bf16[64,1024]{1,0:T(8,128)(2,1)S(1)} collective-permute-done((bf16[64,1024]{1,0:T(8,128)(2,1)S(1)}, bf16[64,1024]{1,0:T(8,128)(2,1)S(1)}, u32[]{:S(2)}, u32[]{:S(2)}) %collective-permute-start.1) | collective-permute-done | bytes 131104 | tf_op jit(solution)/shard_map/ppermute | solution.py:43
  11.9 2.7 %collective-permute-start.3 = (bf16[64,1024]{1,0:T(8,128)(2,1)S(1)}, bf16[64,1024]{1,0:T(8,128)(2,1)S(1)}, u32[]{:S(2)}, u32[]{:S(2)}) collective-permute-start(bf16[64,1024]{1,0:T(8,128)(2,1)S(1)} %pair_sum.2), channel_id=1, source_target_pairs={{0,2},{1,3},{2,0},{3,1},{4,6},{5,7},{6,4},{7,5},{8,10},{9,11},{10,... | collective-permute-start | bytes 393224 | tf_op jit(solution)/shard_map/ppermute | solution.py:43
  14.6 0.9 %send.3 = (bf16[64,1024]{1,0:T(8,128)(2,1)S(1)}, bf16[64,2048]{1,0:T(8,128)(2,1)S(1)}) custom-call(bf16[32,2048]{1,0:T(8,128)(2,1)S(1)} %collective-permute-done.2.here, bf16[32,2048]{1,0:T(8,128)(2,1)S(1)} %collective-permute-done.4.beside, f32[1,2048]{1,0:T(1,128)S(1)} %get-tuple-element.29.b_dec, bf16[2048,1024]{1,0:T(8,128)(2,1)S(1)} %get-tuple-element.30.held), custom_call_target="tpu_custom_call" | custom-call | flops 268435456 | bytes 262144 | tf_op jit(solution)/shard_map/send/pallas_call | solution.py:172
  15.5 1.6 %collective-permute-start.5 = (bf16[64,1024]{1,0:T(8,128)(2,1)S(1)}, bf16[64,1024]{1,0:T(8,128)(2,1)S(1)}, u32[]{:S(2)}, u32[]{:S(2)}) collective-permute-start(bf16[64,1024]{1,0:T(8,128)(2,1)S(1)} %get-tuple-element.40), channel_id=1, source_target_pairs={{0,1},{1,0},{2,3},{3,2},{4,5},{5,4},{6,7},{7,6},{8,9},{9,8},{10,11... | collective-permute-start | bytes 393224 | tf_op jit(solution)/shard_map/ppermute | solution.py:43
  17.1 0.8 %keep.1._.kept = f32[64,1024]{1,0:T(8,128)S(1)} custom-call(bf16[64,2048]{1,0:T(8,128)(2,1)S(1)} %get-tuple-element.37.x, bf16[2048,1024]{1,0:T(8,128)(2,1)S(1)} %get-tuple-element.38.held), custom_call_target="tpu_custom_call" | custom-call | flops 268435456 | bytes 262144 | tf_op jit(solution)/shard_map/keep/pallas_call | solution.py:185
  18.0 3.4 %load_half.2.refs_8_.refs_7_ = f32[1024,2048]{1,0:T(8,128)S(1)} custom-call(f32[64,1024]{1,0:T(8,128)S(1)} %keep.1._.kept, f32[2048,2048]{1,0:T(8,128)} %source.3), custom_call_target="tpu_custom_call" | custom-call | bytes 33554432 | tf_op jit(solution)/shard_map/load_half/pallas_call | solution.py:267
  21.9 0.7 %collective-permute-start.8 = (bf16[64,1024]{1,0:T(8,128)(2,1)S(1)}, bf16[64,1024]{1,0:T(8,128)(2,1)S(1)}, u32[]{:S(2)}, u32[]{:S(2)}) collective-permute-start(bf16[64,1024]{1,0:T(8,128)(2,1)S(1)} %codes.2._.here.refs_0_), channel_id=1, source_target_pairs={{0,8},{4,12},{8,0},{12,4},{1,9},{5,13},{9,1},{13,5},{2,10},{6,14},... | collective-permute-start | bytes 393224 | tf_op jit(solution)/shard_map/ppermute | solution.py:43
  23.3 2.4 %collective-permute-start.6 = (bf16[64,1024]{1,0:T(8,128)(2,1)S(1)}, bf16[64,1024]{1,0:T(8,128)(2,1)S(1)}, u32[]{:S(2)}, u32[]{:S(2)}) collective-permute-start(bf16[64,1024]{1,0:T(8,128)(2,1)S(1)} %codes.2._.here.refs_0_), channel_id=1, source_target_pairs={{0,1},{1,0},{2,3},{3,2},{4,5},{5,4},{6,7},{7,6},{8,9},{9,8},{10,11... | collective-permute-start | bytes 393224 | tf_op jit(solution)/shard_map/ppermute | solution.py:43
  25.8 3.4 %load_half.3.refs_9_.refs_8_ = f32[1024,2048]{1,0:T(8,128)S(1)} custom-call(bf16[64,1024]{1,0:T(8,128)(2,1)S(1)} %codes.2._.here.refs_0_, f32[2048,2048]{1,0:T(8,128)} %source.3), custom_call_target="tpu_custom_call" | custom-call | bytes 33554432 | tf_op jit(solution)/shard_map/load_half/pallas_call | solution.py:267
  29.3 1.3 %collective-permute-done.7.far = bf16[64,1024]{1,0:T(8,128)(2,1)S(1)} collective-permute-done((bf16[64,1024]{1,0:T(8,128)(2,1)S(1)}, bf16[64,1024]{1,0:T(8,128)(2,1)S(1)}, u32[]{:S(2)}, u32[]{:S(2)}) %collective-permute-start.7) | collective-permute-done | bytes 131104 | tf_op jit(solution)/shard_map/ppermute | solution.py:43
  30.8 1.4 %collective-permute-start.11 = (bf16[64,1024]{1,0:T(8,128)(2,1)S(1)}, bf16[64,1024]{1,0:T(8,128)(2,1)S(1)}, u32[]{:S(2)}, u32[]{:S(2)}) collective-permute-start(bf16[64,1024]{1,0:T(8,128)(2,1)S(1)} %codes.3.here.refs_2_), channel_id=1, source_target_pairs={{0,8},{4,12},{8,0},{12,4},{1,9},{5,13},{9,1},{13,5},{2,10},{6,14},... | collective-permute-start | bytes 393224 | tf_op jit(solution)/shard_map/ppermute | solution.py:43
  32.3 0.9 %collective-permute-start.9 = (bf16[64,1024]{1,0:T(8,128)(2,1)S(1)}, bf16[64,1024]{1,0:T(8,128)(2,1)S(1)}, u32[]{:S(2)}, u32[]{:S(2)}) collective-permute-start(bf16[64,1024]{1,0:T(8,128)(2,1)S(1)} %codes.3.here.refs_2_), channel_id=1, source_target_pairs={{0,1},{1,0},{2,3},{3,2},{4,5},{5,4},{6,7},{7,6},{8,9},{9,8},{10,11... | collective-permute-start | bytes 393224 | tf_op jit(solution)/shard_map/ppermute | solution.py:43
  33.1 1.6 %collective-permute-done.10.there = bf16[64,1024]{1,0:T(8,128)(2,1)S(1)} collective-permute-done((bf16[64,1024]{1,0:T(8,128)(2,1)S(1)}, bf16[64,1024]{1,0:T(8,128)(2,1)S(1)}, u32[]{:S(2)}, u32[]{:S(2)}) %collective-permute-start.10) | collective-permute-done | bytes 131104 | tf_op jit(solution)/shard_map/ppermute | solution.py:43
  34.8 1.1 %collective-permute-done.11.there = bf16[64,1024]{1,0:T(8,128)(2,1)S(1)} collective-permute-done((bf16[64,1024]{1,0:T(8,128)(2,1)S(1)}, bf16[64,1024]{1,0:T(8,128)(2,1)S(1)}, u32[]{:S(2)}, u32[]{:S(2)}) %collective-permute-start.11) | collective-permute-done | bytes 131104 | tf_op jit(solution)/shard_map/ppermute | solution.py:43
  36.5 0.8 %collective-permute-done.9.refs_3_ = bf16[64,1024]{1,0:T(8,128)(2,1)S(1)} collective-permute-done((bf16[64,1024]{1,0:T(8,128)(2,1)S(1)}, bf16[64,1024]{1,0:T(8,128)(2,1)S(1)}, u32[]{:S(2)}, u32[]{:S(2)}) %collective-permute-start.9) | collective-permute-done | bytes 131104 | tf_op jit(solution)/shard_map/ppermute | solution.py:43
  37.5 0.7 %collective-permute-start.15 = (bf16[64,1024]{1,0:T(8,128)(2,1)S(1)}, bf16[64,1024]{1,0:T(8,128)(2,1)S(1)}, u32[]{:S(2)}, u32[]{:S(2)}) collective-permute-start(bf16[64,1024]{1,0:T(8,128)(2,1)S(1)} %next_column.1), channel_id=1, source_target_pairs={{0,1},{1,0},{2,3},{3,2},{4,5},{5,4},{6,7},{7,6},{8,9},{9,8},{10,11... | collective-permute-start | bytes 393224 | tf_op jit(solution)/shard_map/ppermute | solution.py:43
  38.2 3.7 %gram.2.refs_9_ = f32[2048,2048]{1,0:T(8,128)} custom-call(bf16[64,1024]{1,0:T(8,128)(2,1)S(1)} %codes.2._.here.refs_0_, bf16[64,1024]{1,0:T(8,128)(2,1)S(1)} %collective-permute-done.6.here.refs_1_, bf16[64,1024]{1,0:T(8,128)(2,1)S(1)} %codes.3.here.refs_2_, bf16[64,1024]{1,0:T(8,128)(2,1)S(1)} %collective-permute-done.9.refs_3_, ...), custom_call_target="tpu_custom_call" | custom-call | flops 536870912 | bytes 16777216 | tf_op jit(solution)/shard_map/gram/pallas_call | solution.py:328
  42.0 1.3 %collective-permute-done.15.refs_5_ = bf16[64,1024]{1,0:T(8,128)(2,1)S(1)} collective-permute-done((bf16[64,1024]{1,0:T(8,128)(2,1)S(1)}, bf16[64,1024]{1,0:T(8,128)(2,1)S(1)}, u32[]{:S(2)}, u32[]{:S(2)}) %collective-permute-start.15) | collective-permute-done | bytes 131104 | tf_op jit(solution)/shard_map/ppermute | solution.py:43
  43.3 3.7 %gram.3 = f32[2048,2048]{1,0:T(8,128)} custom-call(bf16[64,1024]{1,0:T(8,128)(2,1)S(1)} %codes.2._.here.refs_0_, bf16[64,1024]{1,0:T(8,128)(2,1)S(1)} %collective-permute-done.6.here.refs_1_, bf16[64,1024]{1,0:T(8,128)(2,1)S(1)} %codes.3.here.refs_2_, bf16[64,1024]{1,0:T(8,128)(2,1)S(1)} %collective-permute-done.9.refs_3_, ...), custom_call_target="tpu_custom_call", output_to_operand_aliasing={{}: (9, {})} | custom-call | flops 536870912 | bytes 16777216 | tf_op jit(solution)/shard_map/gram/pallas_call | solution.py:328
  (27 shorter events, 2.9 us)
Async XLA Ops:
  0.0 5.3 %collective-permute-start = (bf16[32,2048]{1,0:T(8,128)(2,1)}, bf16[32,2048]{1,0:T(8,128)(2,1)S(1)}, u32[]{:S(2)}, u32[]{:S(2)}) collective-permute-start(bf16[32,2048]{1,0:T(8,128)(2,1)} %stored.1), channel_id=1, source_target_pairs={{0,4},{4,0},{8,12},{12,8},{1,5},{5,1},{9,13},{13,9},{2,6},{6,2},{1... | collective-permute-start | bytes 393224 | tf_op jit(solution)/shard_map/ppermute | solution.py:43
  0.5 9.9 %collective-permute-start.2 = (bf16[32,2048]{1,0:T(8,128)(2,1)}, bf16[32,2048]{1,0:T(8,128)(2,1)S(1)}, u32[]{:S(2)}, u32[]{:S(2)}) collective-permute-start(bf16[32,2048]{1,0:T(8,128)(2,1)} %stored.1), channel_id=1, source_target_pairs={{0,8},{4,12},{8,0},{12,4},{1,9},{5,13},{9,1},{13,5},{2,10},{6,14},... | collective-permute-start | bytes 393224 | tf_op jit(solution)/shard_map/ppermute | solution.py:43
  6.2 5.7 %collective-permute-start.1 = (bf16[64,1024]{1,0:T(8,128)(2,1)S(1)}, bf16[64,1024]{1,0:T(8,128)(2,1)S(1)}, u32[]{:S(2)}, u32[]{:S(2)}) collective-permute-start(bf16[64,1024]{1,0:T(8,128)(2,1)S(1)} %get-tuple-element.33), channel_id=1, source_target_pairs={{0,1},{1,0},{2,3},{3,2},{4,5},{5,4},{6,7},{7,6},{8,9},{9,8},{10,11... | collective-permute-start | bytes 393224 | tf_op jit(solution)/shard_map/ppermute | solution.py:43
  10.4 4.2 %collective-permute-start.4 = (bf16[32,2048]{1,0:T(8,128)(2,1)S(1)}, bf16[32,2048]{1,0:T(8,128)(2,1)S(1)}, u32[]{:S(2)}, u32[]{:S(2)}) collective-permute-start(bf16[32,2048]{1,0:T(8,128)(2,1)S(1)} %collective-permute-done.2.here), channel_id=1, source_target_pairs={{0,4},{4,0},{8,12},{12,8},{1,5},{5,1},{9,13},{13,9},{2,6},{6,2},{1... | collective-permute-start | bytes 393224 | tf_op jit(solution)/shard_map/ppermute | solution.py:43
  11.9 9.5 %collective-permute-start.3 = (bf16[64,1024]{1,0:T(8,128)(2,1)S(1)}, bf16[64,1024]{1,0:T(8,128)(2,1)S(1)}, u32[]{:S(2)}, u32[]{:S(2)}) collective-permute-start(bf16[64,1024]{1,0:T(8,128)(2,1)S(1)} %pair_sum.2), channel_id=1, source_target_pairs={{0,2},{1,3},{2,0},{3,1},{4,6},{5,7},{6,4},{7,5},{8,10},{9,11},{10,... | collective-permute-start | bytes 393224 | tf_op jit(solution)/shard_map/ppermute | solution.py:43
  15.5 6.3 %collective-permute-start.5 = (bf16[64,1024]{1,0:T(8,128)(2,1)S(1)}, bf16[64,1024]{1,0:T(8,128)(2,1)S(1)}, u32[]{:S(2)}, u32[]{:S(2)}) collective-permute-start(bf16[64,1024]{1,0:T(8,128)(2,1)S(1)} %get-tuple-element.40), channel_id=1, source_target_pairs={{0,1},{1,0},{2,3},{3,2},{4,5},{5,4},{6,7},{7,6},{8,9},{9,8},{10,11... | collective-permute-start | bytes 393224 | tf_op jit(solution)/shard_map/ppermute | solution.py:43
  18.0 3.8 %copy-start = (f32[2048]{0:T(1024)S(1)}, f32[2048]{0:T(1024)}, u32[]{:S(2)}) copy-start(f32[2048]{0:T(1024)} %param.8) | copy-start | bytes 24580
  21.9 7.3 %collective-permute-start.8 = (bf16[64,1024]{1,0:T(8,128)(2,1)S(1)}, bf16[64,1024]{1,0:T(8,128)(2,1)S(1)}, u32[]{:S(2)}, u32[]{:S(2)}) collective-permute-start(bf16[64,1024]{1,0:T(8,128)(2,1)S(1)} %codes.2._.here.refs_0_), channel_id=1, source_target_pairs={{0,8},{4,12},{8,0},{12,4},{1,9},{5,13},{9,1},{13,5},{2,10},{6,14},... | collective-permute-start | bytes 393224 | tf_op jit(solution)/shard_map/ppermute | solution.py:43
  22.6 8.0 %collective-permute-start.7 = (bf16[64,1024]{1,0:T(8,128)(2,1)S(1)}, bf16[64,1024]{1,0:T(8,128)(2,1)S(1)}, u32[]{:S(2)}, u32[]{:S(2)}) collective-permute-start(bf16[64,1024]{1,0:T(8,128)(2,1)S(1)} %pair_sum.3), channel_id=1, source_target_pairs={{0,2},{1,3},{2,0},{3,1},{4,6},{5,7},{6,4},{7,5},{8,10},{9,11},{10,... | collective-permute-start | bytes 393224 | tf_op jit(solution)/shard_map/ppermute | solution.py:43
  23.3 7.4 %collective-permute-start.6 = (bf16[64,1024]{1,0:T(8,128)(2,1)S(1)}, bf16[64,1024]{1,0:T(8,128)(2,1)S(1)}, u32[]{:S(2)}, u32[]{:S(2)}) collective-permute-start(bf16[64,1024]{1,0:T(8,128)(2,1)S(1)} %codes.2._.here.refs_0_), channel_id=1, source_target_pairs={{0,1},{1,0},{2,3},{3,2},{4,5},{5,4},{6,7},{7,6},{8,9},{9,8},{10,11... | collective-permute-start | bytes 393224 | tf_op jit(solution)/shard_map/ppermute | solution.py:43
  29.2 5.6 %collective-permute-start.10 = (bf16[64,1024]{1,0:T(8,128)(2,1)S(1)}, bf16[64,1024]{1,0:T(8,128)(2,1)S(1)}, u32[]{:S(2)}, u32[]{:S(2)}) collective-permute-start(bf16[64,1024]{1,0:T(8,128)(2,1)S(1)} %collective-permute-done.8.there), channel_id=1, source_target_pairs={{0,1},{1,0},{2,3},{3,2},{4,5},{5,4},{6,7},{7,6},{8,9},{9,8},{10,11... | collective-permute-start | bytes 393224 | tf_op jit(solution)/shard_map/ppermute | solution.py:43
  30.8 5.0 %collective-permute-start.11 = (bf16[64,1024]{1,0:T(8,128)(2,1)S(1)}, bf16[64,1024]{1,0:T(8,128)(2,1)S(1)}, u32[]{:S(2)}, u32[]{:S(2)}) collective-permute-start(bf16[64,1024]{1,0:T(8,128)(2,1)S(1)} %codes.3.here.refs_2_), channel_id=1, source_target_pairs={{0,8},{4,12},{8,0},{12,4},{1,9},{5,13},{9,1},{13,5},{2,10},{6,14},... | collective-permute-start | bytes 393224 | tf_op jit(solution)/shard_map/ppermute | solution.py:43
  32.3 5.0 %collective-permute-start.9 = (bf16[64,1024]{1,0:T(8,128)(2,1)S(1)}, bf16[64,1024]{1,0:T(8,128)(2,1)S(1)}, u32[]{:S(2)}, u32[]{:S(2)}) collective-permute-start(bf16[64,1024]{1,0:T(8,128)(2,1)S(1)} %codes.3.here.refs_2_), channel_id=1, source_target_pairs={{0,1},{1,0},{2,3},{3,2},{4,5},{5,4},{6,7},{7,6},{8,9},{9,8},{10,11... | collective-permute-start | bytes 393224 | tf_op jit(solution)/shard_map/ppermute | solution.py:43
  33.1 3.3 %collective-permute-start.13 = (bf16[64,1024]{1,0:T(8,128)(2,1)S(1)}, bf16[64,1024]{1,0:T(8,128)(2,1)S(1)}, u32[]{:S(2)}, u32[]{:S(2)}) collective-permute-start(bf16[64,1024]{1,0:T(8,128)(2,1)S(1)} %choose.3.refs_4_), channel_id=1, source_target_pairs={{0,4},{4,0},{8,12},{12,8},{1,5},{5,1},{9,13},{13,9},{2,6},{6,2},{1... | collective-permute-start | bytes 393224 | tf_op jit(solution)/shard_map/ppermute | solution.py:43
  35.9 1.4 %collective-permute-start.12 = (bf16[64,1024]{1,0:T(8,128)(2,1)S(1)}, bf16[64,1024]{1,0:T(8,128)(2,1)S(1)}, u32[]{:S(2)}, u32[]{:S(2)}) collective-permute-start(bf16[64,1024]{1,0:T(8,128)(2,1)S(1)} %pick.1.picked.refs_5_), channel_id=1, source_target_pairs={{0,4},{4,0},{8,12},{12,8},{1,5},{5,1},{9,13},{13,9},{2,6},{6,2},{1... | collective-permute-start | bytes 393224 | tf_op jit(solution)/shard_map/ppermute | solution.py:43
  36.0 1.5 %collective-permute-start.14 = (bf16[64,1024]{1,0:T(8,128)(2,1)S(1)}, bf16[64,1024]{1,0:T(8,128)(2,1)S(1)}, u32[]{:S(2)}, u32[]{:S(2)}) collective-permute-start(bf16[64,1024]{1,0:T(8,128)(2,1)S(1)} %choose.2.refs_4_), channel_id=1, source_target_pairs={{0,4},{4,0},{8,12},{12,8},{1,5},{5,1},{9,13},{13,9},{2,6},{6,2},{1... | collective-permute-start | bytes 393224 | tf_op jit(solution)/shard_map/ppermute | solution.py:43
  37.5 5.8 %collective-permute-start.15 = (bf16[64,1024]{1,0:T(8,128)(2,1)S(1)}, bf16[64,1024]{1,0:T(8,128)(2,1)S(1)}, u32[]{:S(2)}, u32[]{:S(2)}) collective-permute-start(bf16[64,1024]{1,0:T(8,128)(2,1)S(1)} %next_column.1), channel_id=1, source_target_pairs={{0,1},{1,0},{2,3},{3,2},{4,5},{5,4},{6,7},{7,6},{8,9},{9,8},{10,11... | collective-permute-start | bytes 393224 | tf_op jit(solution)/shard_map/ppermute | solution.py:43

commit v5 on v4

--- a/solution.py
+++ b/solution.py
@@ -397,7 +397,7 @@
     held_other_a = choose(other_a, after(other_x_a, own_b))
     passed_other_a = flip(held_other_a, "row", 1)
     pick_b = pick(own_b, after(own_x_b, held_other_a))
-    passed_b = after(flip(pick_b, "row", 1), other_b, passed_own_a, passed_other_a)
+    passed_b = after(flip(pick_b, "row", 1), other_b)
     column_b = flip(next_column(pick_b, passed_b), "col", 1)
     rows = [own_a, other_a, own_b, other_b]
     old = [old_top, old_bottom]

time: 47.2 us -> 46.8 us (level)
  no operation moved by 1% of the time
where the time goes in v5:
time: 46.8 us; the launch traced here: 46.7 us
  Pallas kernels  22 us (47%)
  starting transfers between devices  16.5 us (35%)
  waiting for transfers between devices  7.95 us (17%)
    ppermute x16, starting transfers between devices, flip(): return lax.ppermute(value, axis, [(i, i ^ bit) for i in range(4)])  16.5 us
    ppermute x16, waiting for transfers between devices, flip(): return lax.ppermute(value, axis, [(i, i ^ bit) for i in range(4)])  7.95 us
    pallas_call x2, Pallas kernels, gram(): pl.pallas_call(functools.partial(gram_kernel, other), out_shape=struct((h...  7.47 us
    pallas_call x2, Pallas kernels, load_half(): pl.pallas_call(functools.partial(load_kernel, part), out_shape=struct((ro...  6.79 us
    pallas_call x1, Pallas kernels, first_keep(): pl.pallas_call(first_keep_kernel, out_shape=(struct((rows, width), F32),...  2.5 us
    pallas_call x1, Pallas kernels, load_first(): pl.pallas_call(load_first_kernel, out_shape=(struct(stored.shape, BF16),...  2.31 us
    pallas_call x2, Pallas kernels, send(): pl.pallas_call(send_kernel, out_shape=(struct((rows, width), BF16), struc...  1.82 us
  transfers between devices with their start and end apart: 16, of which 9 were waited for; matrix products, arithmetic and copies ran while one was open for 0% of the time, Pallas kernels for 35%

profile of v5, /device:TPU:0, one launch (start us, length us, event | category | flops | bytes accessed | tf_op | source)
XLA Modules:
  0.0 46.7 jit_solution(8841905390484739262)
XLA Ops:
  0.5 2.5 %collective-permute-start.2 = (bf16[32,2048]{1,0:T(8,128)(2,1)}, bf16[32,2048]{1,0:T(8,128)(2,1)S(1)}, u32[]{:S(2)}, u32[]{:S(2)}) collective-permute-start(bf16[32,2048]{1,0:T(8,128)(2,1)} %stored.1), channel_id=1, source_target_pairs={{0,8},{4,12},{8,0},{12,4},{1,9},{5,13},{9,1},{13,5},{2,10},{6,14},... | collective-permute-start | bytes 393224 | tf_op jit(solution)/shard_map/ppermute | solution.py:43
  2.9 2.3 %load_first.1 = (bf16[32,2048]{1,0:T(8,128)(2,1)S(1)}, f32[1,2048]{1,0:T(1,128)S(1)}, bf16[2048,1024]{1,0:T(8,128)(2,1)S(1)}) custom-call(bf16[32,2048]{1,0:T(8,128)(2,1)} %stored.1, f32[1,2048]{1,0:T(1,128)} %bitcast.4, bf16[2048,2048]{1,0:T(8,128)(2,1)} %w.3), custom_call_target="tpu_custom_call" | custom-call | bytes 4194304 | tf_op jit(solution)/shard_map/load_first/pallas_call | solution.py:125
  5.3 0.9 %send.2 = (bf16[64,1024]{1,0:T(8,128)(2,1)S(1)}, bf16[64,2048]{1,0:T(8,128)(2,1)S(1)}) custom-call(bf16[32,2048]{1,0:T(8,128)(2,1)S(1)} %get-tuple-element.28.here, bf16[32,2048]{1,0:T(8,128)(2,1)S(1)} %collective-permute-done.beside, f32[1,2048]{1,0:T(1,128)S(1)} %get-tuple-element.29.b_dec, bf16[2048,1024]{1,0:T(8,128)(2,1)S(1)} %get-tuple-element.30.held), custom_call_target="tpu_custom_call" | custom-call | flops 268435456 | bytes 262144 | tf_op jit(solution)/shard_map/send/pallas_call | solution.py:172
  6.2 1.6 %collective-permute-start.1 = (bf16[64,1024]{1,0:T(8,128)(2,1)S(1)}, bf16[64,1024]{1,0:T(8,128)(2,1)S(1)}, u32[]{:S(2)}, u32[]{:S(2)}) collective-permute-start(bf16[64,1024]{1,0:T(8,128)(2,1)S(1)} %get-tuple-element.33), channel_id=1, source_target_pairs={{0,1},{1,0},{2,3},{3,2},{4,5},{5,4},{6,7},{7,6},{8,9},{9,8},{10,11... | collective-permute-start | bytes 393224 | tf_op jit(solution)/shard_map/ppermute | solution.py:43
  7.8 2.5 %first_keep.1 = (f32[64,1024]{1,0:T(8,128)S(1)}, bf16[2048,1024]{1,0:T(8,128)(2,1)S(1)}) custom-call(bf16[64,2048]{1,0:T(8,128)(2,1)S(1)} %get-tuple-element.31.x, bf16[2048,2048]{1,0:T(8,128)(2,1)} %w.3), custom_call_target="tpu_custom_call" | custom-call | flops 268435456 | bytes 4194304 | tf_op jit(solution)/shard_map/first_keep/pallas_call | solution.py:146
  10.4 1.5 %collective-permute-done.1.sent = bf16[64,1024]{1,0:T(8,128)(2,1)S(1)} collective-permute-done((bf16[64,1024]{1,0:T(8,128)(2,1)S(1)}, bf16[64,1024]{1,0:T(8,128)(2,1)S(1)}, u32[]{:S(2)}, u32[]{:S(2)}) %collective-permute-start.1) | collective-permute-done | bytes 131104 | tf_op jit(solution)/shard_map/ppermute | solution.py:43
  11.9 2.7 %collective-permute-start.3 = (bf16[64,1024]{1,0:T(8,128)(2,1)S(1)}, bf16[64,1024]{1,0:T(8,128)(2,1)S(1)}, u32[]{:S(2)}, u32[]{:S(2)}) collective-permute-start(bf16[64,1024]{1,0:T(8,128)(2,1)S(1)} %pair_sum.2), channel_id=1, source_target_pairs={{0,2},{1,3},{2,0},{3,1},{4,6},{5,7},{6,4},{7,5},{8,10},{9,11},{10,... | collective-permute-start | bytes 393224 | tf_op jit(solution)/shard_map/ppermute | solution.py:43
  14.6 0.9 %send.3 = (bf16[64,1024]{1,0:T(8,128)(2,1)S(1)}, bf16[64,2048]{1,0:T(8,128)(2,1)S(1)}) custom-call(bf16[32,2048]{1,0:T(8,128)(2,1)S(1)} %collective-permute-done.2.here, bf16[32,2048]{1,0:T(8,128)(2,1)S(1)} %collective-permute-done.4.beside, f32[1,2048]{1,0:T(1,128)S(1)} %get-tuple-element.29.b_dec, bf16[2048,1024]{1,0:T(8,128)(2,1)S(1)} %get-tuple-element.30.held), custom_call_target="tpu_custom_call" | custom-call | flops 268435456 | bytes 262144 | tf_op jit(solution)/shard_map/send/pallas_call | solution.py:172
  15.5 1.6 %collective-permute-start.5 = (bf16[64,1024]{1,0:T(8,128)(2,1)S(1)}, bf16[64,1024]{1,0:T(8,128)(2,1)S(1)}, u32[]{:S(2)}, u32[]{:S(2)}) collective-permute-start(bf16[64,1024]{1,0:T(8,128)(2,1)S(1)} %get-tuple-element.40), channel_id=1, source_target_pairs={{0,1},{1,0},{2,3},{3,2},{4,5},{5,4},{6,7},{7,6},{8,9},{9,8},{10,11... | collective-permute-start | bytes 393224 | tf_op jit(solution)/shard_map/ppermute | solution.py:43
  17.1 0.8 %keep.1._.kept = f32[64,1024]{1,0:T(8,128)S(1)} custom-call(bf16[64,2048]{1,0:T(8,128)(2,1)S(1)} %get-tuple-element.37.x, bf16[2048,1024]{1,0:T(8,128)(2,1)S(1)} %get-tuple-element.38.held), custom_call_target="tpu_custom_call" | custom-call | flops 268435456 | bytes 262144 | tf_op jit(solution)/shard_map/keep/pallas_call | solution.py:185
  18.0 3.4 %load_half.2.refs_8_.refs_7_ = f32[1024,2048]{1,0:T(8,128)S(1)} custom-call(f32[64,1024]{1,0:T(8,128)S(1)} %keep.1._.kept, f32[2048,2048]{1,0:T(8,128)} %source.3), custom_call_target="tpu_custom_call" | custom-call | bytes 33554432 | tf_op jit(solution)/shard_map/load_half/pallas_call | solution.py:267
  21.9 0.7 %collective-permute-start.8 = (bf16[64,1024]{1,0:T(8,128)(2,1)S(1)}, bf16[64,1024]{1,0:T(8,128)(2,1)S(1)}, u32[]{:S(2)}, u32[]{:S(2)}) collective-permute-start(bf16[64,1024]{1,0:T(8,128)(2,1)S(1)} %codes.2._.here.refs_0_), channel_id=1, source_target_pairs={{0,8},{4,12},{8,0},{12,4},{1,9},{5,13},{9,1},{13,5},{2,10},{6,14},... | collective-permute-start | bytes 393224 | tf_op jit(solution)/shard_map/ppermute | solution.py:43
  22.6 0.7 %collective-permute-start.7 = (bf16[64,1024]{1,0:T(8,128)(2,1)S(1)}, bf16[64,1024]{1,0:T(8,128)(2,1)S(1)}, u32[]{:S(2)}, u32[]{:S(2)}) collective-permute-start(bf16[64,1024]{1,0:T(8,128)(2,1)S(1)} %pair_sum.3), channel_id=1, source_target_pairs={{0,2},{1,3},{2,0},{3,1},{4,6},{5,7},{6,4},{7,5},{8,10},{9,11},{10,... | collective-permute-start | bytes 393224 | tf_op jit(solution)/shard_map/ppermute | solution.py:43
  23.3 2.4 %collective-permute-start.6 = (bf16[64,1024]{1,0:T(8,128)(2,1)S(1)}, bf16[64,1024]{1,0:T(8,128)(2,1)S(1)}, u32[]{:S(2)}, u32[]{:S(2)}) collective-permute-start(bf16[64,1024]{1,0:T(8,128)(2,1)S(1)} %codes.2._.here.refs_0_), channel_id=1, source_target_pairs={{0,1},{1,0},{2,3},{3,2},{4,5},{5,4},{6,7},{7,6},{8,9},{9,8},{10,11... | collective-permute-start | bytes 393224 | tf_op jit(solution)/shard_map/ppermute | solution.py:43
  25.8 3.4 %load_half.3.refs_9_.refs_8_ = f32[1024,2048]{1,0:T(8,128)S(1)} custom-call(bf16[64,1024]{1,0:T(8,128)(2,1)S(1)} %codes.2._.here.refs_0_, f32[2048,2048]{1,0:T(8,128)} %source.3), custom_call_target="tpu_custom_call" | custom-call | bytes 33554432 | tf_op jit(solution)/shard_map/load_half/pallas_call | solution.py:267
  29.3 1.3 %collective-permute-done.7.far = bf16[64,1024]{1,0:T(8,128)(2,1)S(1)} collective-permute-done((bf16[64,1024]{1,0:T(8,128)(2,1)S(1)}, bf16[64,1024]{1,0:T(8,128)(2,1)S(1)}, u32[]{:S(2)}, u32[]{:S(2)}) %collective-permute-start.7) | collective-permute-done | bytes 131104 | tf_op jit(solution)/shard_map/ppermute | solution.py:43
  30.8 1.4 %collective-permute-start.11 = (bf16[64,1024]{1,0:T(8,128)(2,1)S(1)}, bf16[64,1024]{1,0:T(8,128)(2,1)S(1)}, u32[]{:S(2)}, u32[]{:S(2)}) collective-permute-start(bf16[64,1024]{1,0:T(8,128)(2,1)S(1)} %codes.3.here.refs_2_), channel_id=1, source_target_pairs={{0,8},{4,12},{8,0},{12,4},{1,9},{5,13},{9,1},{13,5},{2,10},{6,14},... | collective-permute-start | bytes 393224 | tf_op jit(solution)/shard_map/ppermute | solution.py:43
  32.3 0.8 %collective-permute-start.9 = (bf16[64,1024]{1,0:T(8,128)(2,1)S(1)}, bf16[64,1024]{1,0:T(8,128)(2,1)S(1)}, u32[]{:S(2)}, u32[]{:S(2)}) collective-permute-start(bf16[64,1024]{1,0:T(8,128)(2,1)S(1)} %codes.3.here.refs_2_), channel_id=1, source_target_pairs={{0,1},{1,0},{2,3},{3,2},{4,5},{5,4},{6,7},{7,6},{8,9},{9,8},{10,11... | collective-permute-start | bytes 393224 | tf_op jit(solution)/shard_map/ppermute | solution.py:43
  33.1 1.8 %collective-permute-done.10.there = bf16[64,1024]{1,0:T(8,128)(2,1)S(1)} collective-permute-done((bf16[64,1024]{1,0:T(8,128)(2,1)S(1)}, bf16[64,1024]{1,0:T(8,128)(2,1)S(1)}, u32[]{:S(2)}, u32[]{:S(2)}) %collective-permute-start.10) | collective-permute-done | bytes 131104 | tf_op jit(solution)/shard_map/ppermute | solution.py:43
  34.9 1.0 %collective-permute-done.11.there = bf16[64,1024]{1,0:T(8,128)(2,1)S(1)} collective-permute-done((bf16[64,1024]{1,0:T(8,128)(2,1)S(1)}, bf16[64,1024]{1,0:T(8,128)(2,1)S(1)}, u32[]{:S(2)}, u32[]{:S(2)}) %collective-permute-start.11) | collective-permute-done | bytes 131104 | tf_op jit(solution)/shard_map/ppermute | solution.py:43
  37.3 0.8 %collective-permute-start.13 = (bf16[64,1024]{1,0:T(8,128)(2,1)S(1)}, bf16[64,1024]{1,0:T(8,128)(2,1)S(1)}, u32[]{:S(2)}, u32[]{:S(2)}) collective-permute-start(bf16[64,1024]{1,0:T(8,128)(2,1)S(1)} %next_column.1), channel_id=1, source_target_pairs={{0,1},{1,0},{2,3},{3,2},{4,5},{5,4},{6,7},{7,6},{8,9},{9,8},{10,11... | collective-permute-start | bytes 393224 | tf_op jit(solution)/shard_map/ppermute | solution.py:43
  38.1 3.7 %gram.2.refs_9_ = f32[2048,2048]{1,0:T(8,128)} custom-call(bf16[64,1024]{1,0:T(8,128)(2,1)S(1)} %codes.2._.here.refs_0_, bf16[64,1024]{1,0:T(8,128)(2,1)S(1)} %collective-permute-done.6.here.refs_1_, bf16[64,1024]{1,0:T(8,128)(2,1)S(1)} %codes.3.here.refs_2_, bf16[64,1024]{1,0:T(8,128)(2,1)S(1)} %collective-permute-done.9.refs_3_, ...), custom_call_target="tpu_custom_call" | custom-call | flops 536870912 | bytes 16777216 | tf_op jit(solution)/shard_map/gram/pallas_call | solution.py:328
  41.9 1.1 %collective-permute-done.13.refs_5_ = bf16[64,1024]{1,0:T(8,128)(2,1)S(1)} collective-permute-done((bf16[64,1024]{1,0:T(8,128)(2,1)S(1)}, bf16[64,1024]{1,0:T(8,128)(2,1)S(1)}, u32[]{:S(2)}, u32[]{:S(2)}) %collective-permute-start.13) | collective-permute-done | bytes 131104 | tf_op jit(solution)/shard_map/ppermute | solution.py:43
  42.9 3.7 %gram.3 = f32[2048,2048]{1,0:T(8,128)} custom-call(bf16[64,1024]{1,0:T(8,128)(2,1)S(1)} %codes.2._.here.refs_0_, bf16[64,1024]{1,0:T(8,128)(2,1)S(1)} %collective-permute-done.6.here.refs_1_, bf16[64,1024]{1,0:T(8,128)(2,1)S(1)} %codes.3.here.refs_2_, bf16[64,1024]{1,0:T(8,128)(2,1)S(1)} %collective-permute-done.9.refs_3_, ...), custom_call_target="tpu_custom_call", output_to_operand_aliasing={{}: (9, {})} | custom-call | flops 536870912 | bytes 16777216 | tf_op jit(solution)/shard_map/gram/pallas_call | solution.py:328
  (27 shorter events, 2.8 us)
Async XLA Ops:
  0.0 5.3 %collective-permute-start = (bf16[32,2048]{1,0:T(8,128)(2,1)}, bf16[32,2048]{1,0:T(8,128)(2,1)S(1)}, u32[]{:S(2)}, u32[]{:S(2)}) collective-permute-start(bf16[32,2048]{1,0:T(8,128)(2,1)} %stored.1), channel_id=1, source_target_pairs={{0,4},{4,0},{8,12},{12,8},{1,5},{5,1},{9,13},{13,9},{2,6},{6,2},{1... | collective-permute-start | bytes 393224 | tf_op jit(solution)/shard_map/ppermute | solution.py:43
  0.5 9.9 %collective-permute-start.2 = (bf16[32,2048]{1,0:T(8,128)(2,1)}, bf16[32,2048]{1,0:T(8,128)(2,1)S(1)}, u32[]{:S(2)}, u32[]{:S(2)}) collective-permute-start(bf16[32,2048]{1,0:T(8,128)(2,1)} %stored.1), channel_id=1, source_target_pairs={{0,8},{4,12},{8,0},{12,4},{1,9},{5,13},{9,1},{13,5},{2,10},{6,14},... | collective-permute-start | bytes 393224 | tf_op jit(solution)/shard_map/ppermute | solution.py:43
  6.2 5.7 %collective-permute-start.1 = (bf16[64,1024]{1,0:T(8,128)(2,1)S(1)}, bf16[64,1024]{1,0:T(8,128)(2,1)S(1)}, u32[]{:S(2)}, u32[]{:S(2)}) collective-permute-start(bf16[64,1024]{1,0:T(8,128)(2,1)S(1)} %get-tuple-element.33), channel_id=1, source_target_pairs={{0,1},{1,0},{2,3},{3,2},{4,5},{5,4},{6,7},{7,6},{8,9},{9,8},{10,11... | collective-permute-start | bytes 393224 | tf_op jit(solution)/shard_map/ppermute | solution.py:43
  10.4 4.2 %collective-permute-start.4 = (bf16[32,2048]{1,0:T(8,128)(2,1)S(1)}, bf16[32,2048]{1,0:T(8,128)(2,1)S(1)}, u32[]{:S(2)}, u32[]{:S(2)}) collective-permute-start(bf16[32,2048]{1,0:T(8,128)(2,1)S(1)} %collective-permute-done.2.here), channel_id=1, source_target_pairs={{0,4},{4,0},{8,12},{12,8},{1,5},{5,1},{9,13},{13,9},{2,6},{6,2},{1... | collective-permute-start | bytes 393224 | tf_op jit(solution)/shard_map/ppermute | solution.py:43
  11.9 9.5 %collective-permute-start.3 = (bf16[64,1024]{1,0:T(8,128)(2,1)S(1)}, bf16[64,1024]{1,0:T(8,128)(2,1)S(1)}, u32[]{:S(2)}, u32[]{:S(2)}) collective-permute-start(bf16[64,1024]{1,0:T(8,128)(2,1)S(1)} %pair_sum.2), channel_id=1, source_target_pairs={{0,2},{1,3},{2,0},{3,1},{4,6},{5,7},{6,4},{7,5},{8,10},{9,11},{10,... | collective-permute-start | bytes 393224 | tf_op jit(solution)/shard_map/ppermute | solution.py:43
  15.5 6.3 %collective-permute-start.5 = (bf16[64,1024]{1,0:T(8,128)(2,1)S(1)}, bf16[64,1024]{1,0:T(8,128)(2,1)S(1)}, u32[]{:S(2)}, u32[]{:S(2)}) collective-permute-start(bf16[64,1024]{1,0:T(8,128)(2,1)S(1)} %get-tuple-element.40), channel_id=1, source_target_pairs={{0,1},{1,0},{2,3},{3,2},{4,5},{5,4},{6,7},{7,6},{8,9},{9,8},{10,11... | collective-permute-start | bytes 393224 | tf_op jit(solution)/shard_map/ppermute | solution.py:43
  18.0 3.8 %copy-start = (f32[2048]{0:T(1024)S(1)}, f32[2048]{0:T(1024)}, u32[]{:S(2)}) copy-start(f32[2048]{0:T(1024)} %param.8) | copy-start | bytes 24580
  21.9 7.3 %collective-permute-start.8 = (bf16[64,1024]{1,0:T(8,128)(2,1)S(1)}, bf16[64,1024]{1,0:T(8,128)(2,1)S(1)}, u32[]{:S(2)}, u32[]{:S(2)}) collective-permute-start(bf16[64,1024]{1,0:T(8,128)(2,1)S(1)} %codes.2._.here.refs_0_), channel_id=1, source_target_pairs={{0,8},{4,12},{8,0},{12,4},{1,9},{5,13},{9,1},{13,5},{2,10},{6,14},... | collective-permute-start | bytes 393224 | tf_op jit(solution)/shard_map/ppermute | solution.py:43
  22.6 8.0 %collective-permute-start.7 = (bf16[64,1024]{1,0:T(8,128)(2,1)S(1)}, bf16[64,1024]{1,0:T(8,128)(2,1)S(1)}, u32[]{:S(2)}, u32[]{:S(2)}) collective-permute-start(bf16[64,1024]{1,0:T(8,128)(2,1)S(1)} %pair_sum.3), channel_id=1, source_target_pairs={{0,2},{1,3},{2,0},{3,1},{4,6},{5,7},{6,4},{7,5},{8,10},{9,11},{10,... | collective-permute-start | bytes 393224 | tf_op jit(solution)/shard_map/ppermute | solution.py:43
  23.3 7.4 %collective-permute-start.6 = (bf16[64,1024]{1,0:T(8,128)(2,1)S(1)}, bf16[64,1024]{1,0:T(8,128)(2,1)S(1)}, u32[]{:S(2)}, u32[]{:S(2)}) collective-permute-start(bf16[64,1024]{1,0:T(8,128)(2,1)S(1)} %codes.2._.here.refs_0_), channel_id=1, source_target_pairs={{0,1},{1,0},{2,3},{3,2},{4,5},{5,4},{6,7},{7,6},{8,9},{9,8},{10,11... | collective-permute-start | bytes 393224 | tf_op jit(solution)/shard_map/ppermute | solution.py:43
  29.2 5.7 %collective-permute-start.10 = (bf16[64,1024]{1,0:T(8,128)(2,1)S(1)}, bf16[64,1024]{1,0:T(8,128)(2,1)S(1)}, u32[]{:S(2)}, u32[]{:S(2)}) collective-permute-start(bf16[64,1024]{1,0:T(8,128)(2,1)S(1)} %collective-permute-done.8.there), channel_id=1, source_target_pairs={{0,1},{1,0},{2,3},{3,2},{4,5},{5,4},{6,7},{7,6},{8,9},{9,8},{10,11... | collective-permute-start | bytes 393224 | tf_op jit(solution)/shard_map/ppermute | solution.py:43
  30.8 5.0 %collective-permute-start.11 = (bf16[64,1024]{1,0:T(8,128)(2,1)S(1)}, bf16[64,1024]{1,0:T(8,128)(2,1)S(1)}, u32[]{:S(2)}, u32[]{:S(2)}) collective-permute-start(bf16[64,1024]{1,0:T(8,128)(2,1)S(1)} %codes.3.here.refs_2_), channel_id=1, source_target_pairs={{0,8},{4,12},{8,0},{12,4},{1,9},{5,13},{9,1},{13,5},{2,10},{6,14},... | collective-permute-start | bytes 393224 | tf_op jit(solution)/shard_map/ppermute | solution.py:43
  32.3 5.0 %collective-permute-start.9 = (bf16[64,1024]{1,0:T(8,128)(2,1)S(1)}, bf16[64,1024]{1,0:T(8,128)(2,1)S(1)}, u32[]{:S(2)}, u32[]{:S(2)}) collective-permute-start(bf16[64,1024]{1,0:T(8,128)(2,1)S(1)} %codes.3.here.refs_2_), channel_id=1, source_target_pairs={{0,1},{1,0},{2,3},{3,2},{4,5},{5,4},{6,7},{7,6},{8,9},{9,8},{10,11... | collective-permute-start | bytes 393224 | tf_op jit(solution)/shard_map/ppermute | solution.py:43
  35.9 1.4 %collective-permute-start.12 = (bf16[64,1024]{1,0:T(8,128)(2,1)S(1)}, bf16[64,1024]{1,0:T(8,128)(2,1)S(1)}, u32[]{:S(2)}, u32[]{:S(2)}) collective-permute-start(bf16[64,1024]{1,0:T(8,128)(2,1)S(1)} %pick.1.picked.refs_5_), channel_id=1, source_target_pairs={{0,4},{4,0},{8,12},{12,8},{1,5},{5,1},{9,13},{13,9},{2,6},{6,2},{1... | collective-permute-start | bytes 393224 | tf_op jit(solution)/shard_map/ppermute | solution.py:43
  36.0 2.1 %collective-permute-start.14 = (bf16[64,1024]{1,0:T(8,128)(2,1)S(1)}, bf16[64,1024]{1,0:T(8,128)(2,1)S(1)}, u32[]{:S(2)}, u32[]{:S(2)}) collective-permute-start(bf16[64,1024]{1,0:T(8,128)(2,1)S(1)} %choose.3.refs_4_), channel_id=1, source_target_pairs={{0,4},{4,0},{8,12},{12,8},{1,5},{5,1},{9,13},{13,9},{2,6},{6,2},{1... | collective-permute-start | bytes 393224 | tf_op jit(solution)/shard_map/ppermute | solution.py:43
  37.3 5.6 %collective-permute-start.13 = (bf16[64,1024]{1,0:T(8,128)(2,1)S(1)}, bf16[64,1024]{1,0:T(8,128)(2,1)S(1)}, u32[]{:S(2)}, u32[]{:S(2)}) collective-permute-start(bf16[64,1024]{1,0:T(8,128)(2,1)S(1)} %next_column.1), channel_id=1, source_target_pairs={{0,1},{1,0},{2,3},{3,2},{4,5},{5,4},{6,7},{7,6},{8,9},{9,8},{10,11... | collective-permute-start | bytes 393224 | tf_op jit(solution)/shard_map/ppermute | solution.py:43
  38.1 4.8 %collective-permute-start.15 = (bf16[64,1024]{1,0:T(8,128)(2,1)S(1)}, bf16[64,1024]{1,0:T(8,128)(2,1)S(1)}, u32[]{:S(2)}, u32[]{:S(2)}) collective-permute-start(bf16[64,1024]{1,0:T(8,128)(2,1)S(1)} %choose.2.refs_4_), channel_id=1, source_target_pairs={{0,4},{4,0},{8,12},{12,8},{1,5},{5,1},{9,13},{13,9},{2,6},{6,2},{1... | collective-permute-start | bytes 393224 | tf_op jit(solution)/shard_map/ppermute | solution.py:43
